TPU v7x, 256 devices: a whole 4x4x8 slice. The times are simulated.
256 devices in a mesh: section: 8 (over z_lo, x), expert: 32 (over z_hi, y, core).
Axes of the slice: x: 4, y: 4, z: 8 (z_hi: 4, z_lo: 2; z = z_hi * 2 + z_lo), core: 2. Of those that a mesh axis runs over, the one named last changes fastest.
Arguments:
- queries: bfloat16 [8, 512, 36864], P('section', None, 'expert'), may hold values from -48 to 48
- stretch_latents: bfloat16 [8, 512, 576], P('section', 'expert'), may hold values from -6 to 6
- pool_latents: bfloat16 [8, 3072, 576], P('section', 'expert'), may hold values from -6 to 6
- stretch_offset: int32 [8], P('section'), may hold values from 0 to 3072
- value_up: bfloat16 [8, 64, 512, 128], P('section', 'expert'), may hold values from -0.75 to 0.75
- out_proj: bfloat16 [8, 8192, 7168], P('section', 'expert'), may hold values from -0.25 to 0.25
- resid: bfloat16 [8, 512, 7168], P('section', 'expert'), may hold values from -6 to 6
- norm_gain: float32 [8, 7168], P('section'), may hold values from 0.1 to 1.9
- expert_ids: int32 [8, 512, 2], P('section', 'expert'), may hold values from 0 to 3, all different within a row; in each aligned block of 16 rows (0 to 15, 16 to 31, ..., all dimensions but the last counted through in order) at most 12 rows name the same one
- route_weight: float32 [8, 512, 2], P('section', 'expert'), may hold values from 0.05 to 1
- gate_up: bfloat16 [8, 32, 7168, 2, 128], P('section', 'expert'), may hold values from -0.0625 to 0.0625
- down_proj: bfloat16 [8, 32, 128, 7168], P('section', 'expert'), may hold values from -0.1875 to 0.1875
- page_owner: int32 [8, 32], P('section', 'expert'), may hold values from 0 to 7
Outputs:
- layer_out: bfloat16 [8, 512, 7168], P('section', 'expert')
- page_store: bfloat16 [8, 32, 8, 9216], P('section', 'expert')
Inputs may be any that keep to these rules, and one draw needn't show every extreme that they name: `expert_ids`: in the 16 tokens of one device no expert is named by more than 12 tokens.
All inputs are finite; a program needn't handle non-finite values.
Results may differ from a plain program's by a relative error of at most 0.029.
Values may be sent and summed in bfloat16 or wider, within the bound.
A program may use at most 128 MiB of HBM per device.

v0:
```python
import math

import jax
import jax.numpy as jnp
from jax import lax
from jax.sharding import PartitionSpec as P

LAT = 512
ROPE = 64
LATW = 576
HEAD_DIM = 128
EXP_SPAN = 8
PAGE = 16


def body(
    queries,
    stretch_latents,
    pool_latents,
    stretch_offset,
    value_up,
    out_proj,
    resid,
    norm_gain,
    expert_ids,
    route_weight,
    gate_up,
    down_proj,
    page_owner,
):
    width_all = lax.axis_size("expert")
    sections = lax.axis_size("section")
    query = queries[0]
    stretch_rows = query.shape[0]
    heads_here = value_up.shape[1]
    pool_here = pool_latents.shape[1]
    tok_here = stretch_latents.shape[1]
    row_dev = pool_here + tok_here
    offset = stretch_offset[0]
    query_rows = (
        query.reshape(stretch_rows, heads_here, LATW)
        .transpose(1, 0, 2)
        .reshape(heads_here * stretch_rows, LATW)
    )
    query_tok = jnp.tile(jnp.arange(stretch_rows, dtype=jnp.int32), heads_here)
    scale = 1.0 / math.sqrt(HEAD_DIM + ROPE)
    own_keys = jnp.concatenate([pool_latents[0], stretch_latents[0]], axis=0)
    piece = lax.all_gather(own_keys, "expert", axis=0, tiled=True)
    running = jnp.full((heads_here * stretch_rows,), -1e30, jnp.float32)
    count = piece.shape[0]
    index = jnp.arange(count, dtype=jnp.int32)
    shard = index // row_dev
    local = index % row_dev
    in_pool = local < pool_here
    pool_pos = shard * pool_here + local
    token = shard * tok_here + local - pool_here
    visible = jnp.where(
        in_pool[None, :], (pool_pos < offset)[None, :], token[None, :] <= query_tok[:, None]
    )
    scores = jnp.einsum("qd,kd->qk", query_rows, piece, preferred_element_type=jnp.float32) * scale
    newmax = jnp.maximum(running, jnp.max(jnp.where(visible, scores, -1e30), axis=1))
    probs = jnp.where(visible, jnp.exp(scores - newmax[:, None]), 0.0)
    denom = jnp.sum(probs, axis=1)
    accum = jnp.dot(probs.astype(jnp.bfloat16), piece[:, :LAT], preferred_element_type=jnp.float32)
    running, denom, accum = (newmax, denom, accum)
    latent_out = (
        (accum / denom[:, None]).astype(jnp.bfloat16).reshape(heads_here, stretch_rows, LAT)
    )
    head_out = (
        jnp.einsum("hcl,hld->chd", latent_out, value_up[0], preferred_element_type=jnp.float32)
        .astype(jnp.bfloat16)
        .reshape(stretch_rows, heads_here * HEAD_DIM)
    )
    rows = head_out
    attn = lax.psum_scatter(
        jnp.dot(rows, out_proj[0], preferred_element_type=jnp.float32)
        .astype(jnp.bfloat16)
        .astype(jnp.float32)
        .astype(jnp.bfloat16),
        "expert",
        scatter_dimension=0,
        tiled=True,
    ).astype(jnp.float32)
    mid = resid[0].astype(jnp.float32) + attn
    normed = (
        mid * lax.rsqrt(jnp.mean(mid * mid, axis=-1, keepdims=True) + 1e-06) * norm_gain[0]
    ).astype(jnp.bfloat16)
    scores_r = route_weight[0]
    share = (2.827 * scores_r / jnp.sum(scores_r, axis=-1, keepdims=True)).astype(jnp.bfloat16)
    chosen_ids = expert_ids[0]
    experts_n = width_all // EXP_SPAN
    chosen = (chosen_ids[:, :, None] == jnp.arange(experts_n, dtype=jnp.int32)).astype(jnp.float32)
    weight_in = gate_up[0, 0].reshape(gate_up.shape[2], 2 * gate_up.shape[4])
    hid_here = gate_up.shape[4]
    weight_down = down_proj[0, 0]
    table = jnp.einsum("tke,tk->te", chosen, share.astype(jnp.float32)).astype(jnp.bfloat16)
    everyone, tables = (
        lax.all_gather(normed, "expert", axis=0, tiled=True),
        lax.all_gather(table, "expert", axis=0, tiled=True),
    )
    mine = lax.axis_index("expert") // EXP_SPAN
    factor_all = jnp.sum(
        tables.astype(jnp.float32) * (jnp.arange(experts_n, dtype=jnp.int32) == mine), axis=1
    )
    rows = everyone
    both = jnp.dot(rows, weight_in, preferred_element_type=jnp.float32)
    hidden = (factor_all[:, None] * (jax.nn.silu(both[:, :hid_here]) * both[:, hid_here:])).astype(
        jnp.bfloat16
    )
    moe = lax.psum_scatter(
        jnp.dot(hidden, weight_down, preferred_element_type=jnp.float32)
        .astype(jnp.bfloat16)
        .astype(jnp.float32)
        .astype(jnp.bfloat16),
        "expert",
        scatter_dimension=0,
        tiled=True,
    ).astype(jnp.float32)
    layer_out = (mid + moe).astype(jnp.bfloat16)[None]
    pages_here = tok_here // PAGE
    latent_pages = stretch_latents[0].reshape(pages_here, PAGE * LATW)
    owner_hot = page_owner[0][:, None] == jnp.arange(sections, dtype=jnp.int32)
    outgoing = jnp.where(
        owner_hot[:, :, None], latent_pages[:, None, :], jnp.zeros((), jnp.bfloat16)
    )
    page_store = lax.all_to_all(outgoing, "section", split_axis=1, concat_axis=1, tiled=True)[None]
    return (layer_out, page_store)


def solution(mesh):
    placed = (
        P("section", None, "expert"),
        P("section", "expert", None),
        P("section", "expert", None),
        P("section"),
        P("section", "expert", None, None),
        P("section", "expert", None),
        P("section", "expert", None),
        P("section", None),
        P("section", "expert", None),
        P("section", "expert", None),
        P("section", "expert", None, None, None),
        P("section", "expert", None, None),
        P("section", "expert"),
    )
    return jax.shard_map(
        body,
        mesh=mesh,
        in_specs=placed,
        out_specs=(P("section", "expert", None), P("section", "expert", None, None)),
        check_vma=False,
    )
```

profile of v0, /device:TPU:1, one launch (start us, length us, event | category | flops | bytes accessed | tf_op | source)
XLA Modules:
  0.0 426.0 jit_solution(10739148588657219341)
XLA Ops:
  7.2 0.0 copy-start
  7.2 0.0 all-gather.4.cloned.1.call-start
  7.2 1.7 pad_maximum_fusion
  8.9 0.0 all-gather.4.cloned.1.call-update
  9.0 0.0 reduce-scatter.3.cloned.1.call-start
  9.7 1.6 copy.32
  11.3 1.2 copy.45
  12.5 65.4 %all-gather.4.cloned.1.call-done = bf16[3584,576]{1,0:T(8,128)(2,1)} async-done(((bf16[112,576]{1,0:T(8,128)(2,1)}), bf16[3584,576]{1,0:T(8,128)(2,1)}) %all-gather.4.cloned.1.call-update) | async-done | bytes 4128784 | tf_op jit(solution)/shard_map/all_gather | solution.py:48
  78.0 10.1 %fusion = (f32[1024]{0:T(1024)S(1)}, f32[3584,1024]{1,0:T(8,128)S(1)}) fusion(s32[1024]{0:T(1024)S(1)} %bitcast.86, s32[3584]{0:T(1024)S(1)} %add_add_fusion, pred[3584]{0:T(1024)(128)(4,1)S(1)} %get-tuple-element.4, pred[3584]{0:T(1024)(128)(4,1)S(1)} %get-tuple-element.5, bf16[3584,576]{1,0:T(8,128)(2,1)} %all-gather.4.cloned.1.call-done, ...), kind=kOutput, calls=%fused_computation.2 | convolution fusion | flops 4246207488 | bytes 20018176 | tf_op jit(solution)/shard_map/qd,kd->qk/dot_general | solution.py:60
  88.1 0.0 copy-start.9
  88.1 6.0 %fusion.3 = f32[1024]{0:T(1024)S(1)} fusion(f32[3584,1024]{1,0:T(8,128)S(1)} %get-tuple-element.3, f32[1024]{0:T(1024)S(1)} %broadcast_maximum_fusion, s32[1024]{0:T(1024)S(1)} %bitcast.87, s32[3584]{0:T(1024)S(1)} %add_add_fusion, pred[3584]{0:T(1024)(128)(4,1)S(1)} %get-tuple-element.4, pred[3584]{0:T(1024)(128)(4,1)S(1)} %get-tuple-element.5), kind=kLoop, calls=%fused_computation.8 | loop fusion | flops 22019072 | bytes 14713856 | tf_op jit(solution)/shard_map/reduce_sum | solution.py:63
  94.1 0.0 copy-done.9
  94.2 0.0 copy-start.4
  94.2 0.0 copy-start.1
  94.2 6.6 %divide_convert_fusion = bf16[1024,512]{1,0:T(8,128)(2,1)S(1)} fusion(f32[1024]{0:T(1024)S(1)} %fusion.3, bf16[3584,576]{1,0:T(8,128)(2,1)S(1)} %copy-done.9, f32[3584,1024]{1,0:T(8,128)S(1)} %get-tuple-element.3, f32[1024]{0:T(1024)S(1)} %broadcast_maximum_fusion, s32[1024]{0:T(1024)S(1)} %bitcast.88, s32[3584]{0:T(1024)S(1)} %add_add_fusion, ...), kind=kOutput, calls=%fused_computation.19 | convolution fusion | flops 3781165056 | bytes 19435520 | tf_op jit(solution)/shard_map/dot_general | solution.py:64
  100.8 0.0 copy-done.4
  100.8 0.5 convolution_convert_fusion.2
  101.3 0.0 copy-done.1
  101.3 5.1 %convolution_convert_fusion.1 = bf16[512,7168]{1,0:T(8,128)(2,1)} fusion(bf16[512,256]{0,1:T(8,128)(2,1)S(1)} %bitcast.81, bf16[1,256,7168]{2,1,0:T(8,128)(2,1)S(1)} %copy-done.1), kind=kOutput, calls=%fused_computation.7 | convolution fusion | flops 1882718208 | bytes 11272192 | tf_op jit(solution)/shard_map/dot_general | solution.py:76
  106.4 0.0 copy-start.2
  106.4 0.0 copy-start.6
  106.4 0.0 copy-start.7
  106.4 0.0 copy-start.8
  106.4 0.0 reduce-scatter.3.cloned.1.call-update
  106.4 0.0 all-gather.6.cloned.1.call-start
  106.4 111.7 %reduce-scatter.3.cloned.1.call-done = bf16[16,7168]{1,0:T(8,128)(2,1)} async-done(((bf16[512,7168]{1,0:T(8,128)(2,1)}), bf16[16,7168]{1,0:T(8,128)(2,1)}) %reduce-scatter.3.cloned.1.call-update) | async-done | bytes 229392 | tf_op jit(solution)/shard_map/reduce_scatter | solution.py:75
  218.1 0.0 copy-done.2
  218.2 1.1 multiply_reduce_fusion
  219.3 0.0 copy-done.6
  219.3 1.7 multiply_convert_fusion
  221.0 0.0 all-gather.6.cloned.1.call-update
  221.1 0.0 reduce-scatter.5.cloned.1.call-start
  221.1 0.0 copy-done.7
  221.2 0.1 copy.44
  221.2 0.0 copy-done.8
  221.2 0.1 copy.35
  221.3 0.1 fusion.28
  221.5 0.1 copy.48
  221.5 44.2 %all-gather = bf16[32,16,4]{1,2,0:T(4,128)(2,1)S(1)} all-gather(bf16[1,16,4]{1,2,0:T(4,128)(2,1)S(1)} %bitcast.89), channel_id=1, replica_groups=mesh['section'=8,'expert'=32] {'expert'}, dimensions={0}, use_global_device_ids=true | all-gather | bytes 4224 | tf_op jit(solution)/shard_map/all_gather | solution.py:99
  265.7 0.1 copy.36
  265.8 0.1 copy.37
  265.9 0.1 reshape.134
  266.0 0.1 multiply_reduce_fusion.1
  266.1 27.2 %all-gather.6.cloned.1.call-done = bf16[512,7168]{1,0:T(8,128)(2,1)} async-done(((bf16[16,7168]{1,0:T(8,128)(2,1)}), bf16[512,7168]{1,0:T(8,128)(2,1)}) %all-gather.6.cloned.1.call-update) | async-done | bytes 7340048 | tf_op jit(solution)/shard_map/all_gather | solution.py:98
  293.3 6.2 %fusion.10 = f32[512,256]{1,0:T(8,128)S(1)} fusion(bf16[512,7168]{1,0:T(8,128)(2,1)} %all-gather.6.cloned.1.call-done, bf16[896,8,2,128]{3,2,1,0:T(2,128)(2,1)} %bitcast.91), kind=kOutput, calls=%fused_computation.14 | convolution fusion | flops 1879048192 | bytes 11534336 | tf_op jit(solution)/shard_map/dot_general | solution.py:106
  299.5 0.0 copy-done
  299.5 5.1 %convolution_convert_fusion = bf16[512,7168]{1,0:T(8,128)(2,1)} fusion(bf16[1,1,128,7168]{3,2,1,0:T(8,128)(2,1)S(1)} %copy-done, f32[512,256]{1,0:T(8,128)S(1)} %fusion.10, f32[512]{0:T(512)S(1)} %multiply_reduce_fusion.1), kind=kOutput, calls=%fused_computation.6 | convolution fusion | flops 943652864 | bytes 9701376 | tf_op jit(solution)/shard_map/dot_general | solution.py:111
  304.6 0.0 copy-start.5
  304.6 0.0 copy-start.3
  304.6 0.0 reduce-scatter.5.cloned.1.call-update
  304.6 0.7 copy-done.5
  305.3 0.1 broadcast_in_dim.73
  306.1 0.3 fusion.39
  306.4 0.5 broadcast.194
  306.9 1.5 reduce.3
  308.4 0.1 reshape.137
  308.5 10.4 %all_to_all.5 = bf16[8,2,4608]{2,1,0:T(2,128)(2,1)S(1)} all-to-all(bf16[8,2,4608]{2,1,0:T(2,128)(2,1)S(1)} %reshape.137), channel_id=1, replica_groups=mesh['section'=8,'expert'=32] {'section'}, dimensions={0} | all-to-all | bytes 294912 | tf_op jit(solution)/shard_map/all_to_all | solution.py:126
  318.9 0.1 reshape.138
  319.0 0.7 copy.54
  319.7 98.1 %reduce-scatter.5.cloned.1.call-done = bf16[16,7168]{1,0:T(8,128)(2,1)} async-done(((bf16[512,7168]{1,0:T(8,128)(2,1)}), bf16[16,7168]{1,0:T(8,128)(2,1)}) %reduce-scatter.5.cloned.1.call-update) | async-done | bytes 229392 | tf_op jit(solution)/shard_map/reduce_scatter | solution.py:110
  417.8 0.0 copy-done.3
  417.8 1.7 fusion.19
  (10 shorter events, 0.1 us)
Async XLA Ops:
  7.2 292.3 %copy-start = (bf16[1,1,128,7168]{3,2,1,0:T(8,128)(2,1)S(1)}, bf16[1,1,128,7168]{3,2,1,0:T(8,128)(2,1)}, u32[]{:S(2)}) copy-start(bf16[1,1,128,7168]{3,2,1,0:T(8,128)(2,1)} %param.24) | copy-start | bytes 5505028
  7.2 70.8 %all-gather.4.cloned.1.call-start = ((), (), s32[]{:S(2)}) async-start(), calls=%async_computation.3 | async-start | bytes 4730880 | tf_op jit(solution)/shard_map/all_gather | solution.py:48
  9.0 209.2 %reduce-scatter.3.cloned.1.call-start = ((), (), s32[]{:S(2)}) async-start(), calls=%async_computation.4 | async-start | bytes 7569408 | tf_op jit(solution)/shard_map/reduce_scatter | solution.py:75
  88.1 6.0 %copy-start.9 = (bf16[3584,576]{1,0:T(8,128)(2,1)S(1)}, bf16[3584,576]{1,0:T(8,128)(2,1)}, u32[]{:S(2)}) copy-start(bf16[3584,576]{1,0:T(8,128)(2,1)} %all-gather.4.cloned.1.call-done) | copy-start | bytes 12386308
  94.2 6.6 %copy-start.4 = (bf16[1,2,512,128]{3,2,1,0:T(8,128)(2,1)S(1)}, bf16[1,2,512,128]{3,2,1,0:T(8,128)(2,1)}, u32[]{:S(2)}) copy-start(bf16[1,2,512,128]{3,2,1,0:T(8,128)(2,1)} %param.17) | copy-start | bytes 786436
  94.2 7.1 %copy-start.1 = (bf16[1,256,7168]{2,1,0:T(8,128)(2,1)S(1)}, bf16[1,256,7168]{2,1,0:T(8,128)(2,1)}, u32[]{:S(2)}) copy-start(bf16[1,256,7168]{2,1,0:T(8,128)(2,1)} %param.18) | copy-start | bytes 11010052
  106.4 111.8 %copy-start.2 = (bf16[1,16,7168]{2,1,0:T(8,128)(2,1)S(1)}, bf16[1,16,7168]{2,1,0:T(8,128)(2,1)}, u32[]{:S(2)}) copy-start(bf16[1,16,7168]{2,1,0:T(8,128)(2,1)} %param.19) | copy-start | bytes 688132
  106.4 112.9 %copy-start.6 = (f32[1,7168]{1,0:T(1,128)S(1)}, f32[1,7168]{1,0:T(1,128)}, u32[]{:S(2)}) copy-start(f32[1,7168]{1,0:T(1,128)} %param.20) | copy-start | bytes 86020
  106.4 114.8 %copy-start.7 = (f32[1,16,2]{1,2,0:T(2,128)S(1)}, f32[1,16,2]{1,2,0:T(2,128)}, u32[]{:S(2)}) copy-start(f32[1,16,2]{1,2,0:T(2,128)} %param.22) | copy-start | bytes 388
  106.4 114.9 %copy-start.8 = (s32[1,16,2]{1,2,0:T(2,128)S(1)}, s32[1,16,2]{1,2,0:T(2,128)}, u32[]{:S(2)}) copy-start(s32[1,16,2]{1,2,0:T(2,128)} %param.21) | copy-start | bytes 388
  106.4 186.9 %all-gather.6.cloned.1.call-start = ((), (), s32[]{:S(2)}) async-start(), calls=%async_computation.5 | async-start | bytes 7569408 | tf_op jit(solution)/shard_map/all_gather | solution.py:98
  221.1 196.7 %reduce-scatter.5.cloned.1.call-start = ((), (), s32[]{:S(2)}) async-start(), calls=%async_computation.6 | async-start | bytes 7569408 | tf_op jit(solution)/shard_map/reduce_scatter | solution.py:110
  304.6 0.7 copy-start.5
  304.6 113.1 %copy-start.3 = (bf16[16,7168]{1,0:T(8,128)(2,1)S(1)}, bf16[16,7168]{1,0:T(8,128)(2,1)}, u32[]{:S(2)}) copy-start(bf16[16,7168]{1,0:T(8,128)(2,1)} %reduce-scatter.3.cloned.1.call-done) | copy-start | bytes 688132
Sparse Core Ops, SparseCore 0:
  11.2 66.7 all-gather.3
  106.5 111.5 reduce-scatter.2
  221.6 71.6 all-gather.5
  304.8 112.9 reduce-scatter.4
where the time goes:
time: 426 us
  waiting for transfers between devices  302 us (71%)
  blocking collectives  54.5 us (13%)
  matrix products  33.5 us (8%)
  between operations  15.3 us (4%)
  other arithmetic  14.4 us (3%)
  local copies, waits for them, and re-layouts  5.62 us (1%)
    reduce_scatter x1, waiting for transfers between devices, body(): lax.psum_scatter(jnp.dot(rows, out_proj[0], preferred_element_type=jnp.fl...  112 us
    reduce_scatter x1, waiting for transfers between devices, body(): lax.psum_scatter(jnp.dot(hidden, weight_down, preferred_element_type=jnp....  98.1 us
    all_gather x1, waiting for transfers between devices, body(): piece = lax.all_gather(own_keys, 'expert', axis=0, tiled=True)  65.4 us
    all_gather x1, blocking collectives, body(): lax.all_gather(table, 'expert', axis=0, tiled=True)  44.2 us
    all_gather x1, waiting for transfers between devices, body(): lax.all_gather(normed, 'expert', axis=0, tiled=True)  27.2 us
    all_to_all x1, blocking collectives, body(): lax.all_to_all(outgoing, 'section', split_axis=1, concat_axis=1, tiled=True)  10.4 us
    dot_general x1, matrix products, body(): jnp.einsum('qd,kd->qk', query_rows, piece, preferred_element_type=jnp.flo...  10.1 us
  transfers between devices with their start and end apart: 4, of which 4 were waited for; matrix products, arithmetic and copies ran while one was open for 2% of the time, Pallas kernels for 0%

commit v1 on v0

v1 whole, which is shorter than its diff:
```python
import math

import jax
import jax.numpy as jnp
from jax import lax
from jax.experimental import pallas as pl
from jax.experimental.pallas import tpu as pltpu
from jax.sharding import PartitionSpec as P

MESH = pl.DeviceIdType.MESH
BF = jnp.bfloat16
F32 = jnp.float32
D = 7168
HALF = D // 2
QUART = D // 4
LAT = 512
LATW = 576
WIDE = 640
HEAD_DIM = 128
POOL_DEV = 96
TOK = 16
BLK = POOL_DEV + TOK
STRETCH = 512
CAP = 12
SLOTS = 2 * CAP
ROWS = 2 * SLOTS
TILE = 256
GROUP = 4 * 2 * BLK
NSEC = 8
NEG = -1e30
SCORE = math.log2(math.e) / math.sqrt(192.0)

N_KEY = 31
N_MOE = 32


def one_hot(mask):
    return jnp.where(mask, 1.0, 0.0).astype(BF)


def kernel(
    offset_ref, owner_ref, query_ref, stretch_ref, pool_ref, vup_ref, wo_ref, resid_ref, gain_ref,
    ids_ref, rw_ref, gu_ref, wd_ref,
    out_ref, pages_ref,
    q_raw, qs, keys, acc, ms, ls, ho, wo, wd, gu_raw, w_in, vup, res, gain,
    page_out, part, r_opp, r_rel, r_pure, z_out, z_opp, z_rel, z_pure,
    mid, normed, ss, d_top, d_bot, disp, relay, got, hid,
    dpart, e_opp, e_rel, e_pure, e_out, e_relay, e_got, o_stage,
    load_sem, key_s, key_r, key_x, w_s, w_r, ho_s, ho_r, page_s, page_r,
    ry_s, ry_r, rz_s, rz_r, ss_s, ss_r, moe_s, moe_r, moe_x, rel_r, hid_s, hid_r,
    ey_s, ey_r, ez_s, ez_r, o_s, o_r,
):
    sec = lax.axis_index("section")
    me = lax.axis_index("expert")
    z = me // 8
    y = (me // 2) % 4
    c = me % 2
    d = 1 - 2 * c
    yp, ym, yo = (y + d + 4) % 4, (y - d + 4) % 4, (y + 2) % 4
    zp, zm, zo = (z + d + 4) % 4, (z - d + 4) % 4, (z + 2) % 4

    def dev(zz, yy, cc):
        return (sec, (zz * 4 + yy) * 2 + cc)

    y_plus, y_minus = dev(z, yp, c), dev(z, ym, c)
    z_plus, z_minus = dev(zp, y, c), dev(zm, y, c)
    twin = dev(z, y, 1 - c)
    barrier = pltpu.get_barrier_semaphore()
    for to in (y_plus, y_minus, z_plus, z_minus, twin):
        pl.semaphore_signal(barrier, inc=1, device_id=to, device_id_type=MESH)
    for k in range(1, NSEC):
        pl.semaphore_signal(barrier, inc=1, device_id=((sec + k) % NSEC, me), device_id_type=MESH)

    def remote(src, dst, s_sem, r_sem, to):
        return pltpu.make_async_remote_copy(
            src_ref=src, dst_ref=dst, send_sem=s_sem, recv_sem=r_sem, device_id=to, device_id_type=MESH
        )

    sent = []

    def send(src, dst, s_sem, r_sem, to):
        copy = remote(src, dst, s_sem, r_sem, to)
        copy.start()
        sent.append(copy)

    def arrived(dst, r_sem):
        remote(dst, dst, r_sem, r_sem, twin).wait_recv()

    half_c = pl.ds(pl.multiple_of(c * HALF, 128), HALF)
    half_x = pl.ds(pl.multiple_of((1 - c) * HALF, 128), HALF)

    loads = [
        pltpu.make_async_copy(query_ref, q_raw, load_sem.at[0]),
        pltpu.make_async_copy(vup_ref, vup, load_sem.at[1]),
        pltpu.make_async_copy(wo_ref.at[:, half_c], wo.at[c], load_sem.at[2]),
        pltpu.make_async_copy(gu_ref, gu_raw, load_sem.at[3]),
        pltpu.make_async_copy(wd_ref.at[:, half_c], wd.at[c], load_sem.at[4]),
        pltpu.make_async_copy(resid_ref.at[:, half_c], res.at[c], load_sem.at[5]),
        pltpu.make_async_copy(gain_ref.at[:, half_c], gain, load_sem.at[6]),
    ]
    for load in loads:
        load.start()

    lane16 = lax.broadcasted_iota(jnp.int32, (16, 128), 1)
    sub16 = lax.broadcasted_iota(jnp.int32, (16, 128), 0)
    weights = rw_ref[...]
    total = weights[0:1] + weights[1:2]
    share0 = (2.827 * weights[0:1] / total).astype(BF).astype(F32)
    share1 = (2.827 * weights[1:2] / total).astype(BF).astype(F32)
    ids = ids_ref[...]
    which = lax.broadcasted_iota(jnp.int32, (16, TOK), 0)
    table = jnp.where(ids[0:1] == which, share0, 0.0) + jnp.where(ids[1:2] == which, share1, 0.0)
    place = one_hot(lane16 == sub16 + 64 + 16 * c)
    tab = jnp.dot(table.astype(BF), place, preferred_element_type=F32).astype(BF)
    mine = pl.ds(pl.multiple_of(c * BLK, 16), BLK)
    first = pl.ds(pl.multiple_of(c * BLK, 16), POOL_DEV)
    last = pl.ds(pl.multiple_of(c * BLK + POOL_DEV, 16), TOK)
    keys[z, y, first, 512:WIDE] = jnp.zeros((POOL_DEV, 128), BF)
    keys[z, y, last, 512:WIDE] = tab
    keys[z, y, first, 0:LATW] = pool_ref[...]
    keys[z, y, last, 0:LATW] = stretch_ref[...]
    latents = stretch_ref[...]
    for g in range(NSEC):
        page_out[g] = jnp.where(owner_ref[0] == g, latents, jnp.zeros_like(latents))

    pl.semaphore_wait(barrier, 5 + NSEC - 1)

    def block(zz, yy):
        return keys.at[zz, yy, mine]

    def key_send(zz, yy, number, to):
        remote(block(zz, yy), block(zz, yy), key_s.at[number], key_r.at[zz, yy], to).start()

    def key_twin(zz, yy, number):
        remote(block(zz, yy), block(zz, yy), key_s.at[number], key_x.at[zz, yy], twin).start()

    def key_wait(zz, yy):
        arrived(block(zz, yy), key_r.at[zz, yy])

    def key_twin_wait(zz, yy):
        theirs = keys.at[zz, yy, pl.ds(pl.multiple_of((1 - c) * BLK, 16), BLK)]
        arrived(theirs, key_x.at[zz, yy])

    key_send(z, y, 0, y_plus)
    key_send(z, y, 1, y_minus)
    key_send(z, y, 2, z_plus)
    key_send(z, y, 3, z_minus)
    key_twin(z, y, 4)
    send(wo_ref.at[:, half_x], wo.at[c], w_s.at[0], w_r.at[0], twin)
    send(wd_ref.at[:, half_x], wd.at[c], w_s.at[1], w_r.at[1], twin)
    send(resid_ref.at[:, half_x], res.at[c], w_s.at[2], w_r.at[2], twin)
    for k in range(1, NSEC):
        g = (sec + k) % NSEC
        send(page_out.at[g], pages_ref.at[sec], page_s.at[k - 1], page_r.at[k - 1], (g, me))
    pages_ref[sec] = page_out[sec]

    loads[0].wait()
    lane = lax.broadcasted_iota(jnp.int32, (STRETCH, WIDE), 1)
    qs[0:STRETCH] = jnp.where(lane < LATW, q_raw[:, 0:WIDE], jnp.zeros((), BF))
    row_i = lax.broadcasted_iota(jnp.int32, (WIDE, WIDE), 0)
    col_i = lax.broadcasted_iota(jnp.int32, (WIDE, WIDE), 1)
    shift = one_hot((row_i == col_i + 64) & (col_i < LATW))
    qs[STRETCH:] = jnp.dot(q_raw[:, 512:1152], shift, preferred_element_type=F32).astype(BF)
    acc[...] = jnp.zeros_like(acc)
    ls[...] = jnp.zeros_like(ls)
    ms[...] = jnp.full(ms.shape, NEG, F32)

    def own_column(zz, number):
        key_send(zz, y, number, y_plus)
        key_send(zz, y, number + 1, y_minus)
        key_twin(zz, y, number + 2)

    key_wait(zm, y)
    key_send(zm, y, 5, z_plus)
    own_column(zm, 6)
    key_wait(zp, y)
    own_column(zp, 9)
    key_wait(zo, y)
    own_column(zo, 12)

    offset = offset_ref[0]

    def attend(yy, before):
        r = lax.broadcasted_iota(jnp.int32, (1, GROUP), 1)
        zz = (r >= 2 * BLK).astype(jnp.int32) + (r >= 4 * BLK).astype(jnp.int32) + (r >= 6 * BLK).astype(jnp.int32)
        r = r - zz * (2 * BLK)
        cc = (r >= BLK).astype(jnp.int32)
        r = r - cc * BLK
        owner = zz * 8 + yy * 2 + cc
        seen = jnp.where(owner * POOL_DEV + r < offset, -1, 1 << 20)
        limit = jnp.where(r < POOL_DEV, seen, owner * TOK + r - POOL_DEV)

        def tile(t, carry):
            before(t)
            rows = pl.ds(pl.multiple_of(t * TILE, TILE), TILE)
            part_keys = keys[:, yy].reshape(GROUP, WIDE)
            s = lax.dot_general(qs[rows], part_keys, (((1,), (1,)), ((), ())), preferred_element_type=F32)
            token = (t % 2) * TILE + lax.broadcasted_iota(jnp.int32, (TILE, 1), 0)
            s = jnp.where(limit <= token, s * SCORE, NEG)
            old = ms[rows]
            new = jnp.maximum(old, jnp.max(s, axis=1, keepdims=True))
            p = jnp.exp2(s - new[:, 0:1])
            alpha = jnp.exp2(old - new)
            ms[rows] = new
            ls[rows] = ls[rows] * alpha + jnp.sum(p, axis=1, keepdims=True)
            add = jnp.dot(p.astype(BF), part_keys[:, 0:LAT], preferred_element_type=F32)
            acc[rows] = acc[rows] * alpha[:, 0:1] + add
            return carry

        lax.fori_loop(0, 4, tile, 0)

    def near(t):
        zz = (z - d * t + 8) % 4
        key_wait(zz, ym)
        key_send(zz, ym, 15 + t, y_plus)
        key_twin(zz, ym, 19 + t)
        key_wait(zz, yp)
        key_twin(zz, yp, 23 + t)

    def far(t):
        zz = (z - d * t + 8) % 4
        key_wait(zz, yo)
        key_twin(zz, yo, 27 + t)

    def nothing(t):
        pass

    for zz in (z, zm, zp, zo):
        key_twin_wait(zz, y)
    attend(y, near)
    for zz in (z, zm, zp, zo):
        key_twin_wait(zz, ym)
    attend(ym, far)
    for zz in (z, zm, zp, zo):
        key_twin_wait(zz, yp)
    attend(yp, nothing)
    for zz in (z, zm, zp, zo):
        key_twin_wait(zz, yo)
    attend(yo, nothing)

    loads[1].wait()
    for t in range(4):
        rows = pl.ds(t * TILE, TILE)
        latent = (acc[rows] / ls[rows][:, 0:1]).astype(BF)
        head = jnp.dot(latent, vup[t // 2], preferred_element_type=F32).astype(BF)
        at = (t // 2) * HEAD_DIM
        zs = (t % 2) * 2
        ho[c, zs : zs + 2, :, :, at : at + HEAD_DIM] = head.reshape(2, 4, 32, HEAD_DIM)
    send(ho.at[c], ho.at[c], ho_s.at[0], ho_r.at[0], twin)

    loads[2].wait()
    arrived(wo.at[1 - c], w_r.at[0])
    arrived(ho.at[1 - c], ho_r.at[0])

    def project(yy):
        left = ho[0, :, yy].reshape(128, 2 * HEAD_DIM)
        right = ho[1, :, yy].reshape(128, 2 * HEAD_DIM)

        def column(n, carry):
            cols = pl.ds(pl.multiple_of(n * 896, 128), 896)
            out = jnp.dot(left, wo[0, :, cols], preferred_element_type=F32)
            out = out + jnp.dot(right, wo[1, :, cols], preferred_element_type=F32)
            part[yy, :, :, cols] = out.astype(BF).reshape(4, 32, 896)
            return carry

        lax.fori_loop(0, 4, column, 0)

    order = (zo, zm, zp, z)
    project(yo)
    for k, zz in enumerate(order):
        send(part.at[yo, zz], r_opp.at[k], ry_s.at[k], ry_r.at[k], y_plus)
    project(ym)
    for k, zz in enumerate(order):
        send(part.at[ym, zz], r_pure.at[k], ry_s.at[4 + k], ry_r.at[4 + k], y_minus)
    project(yp)
    project(y)

    loads[3].wait()
    row_p = lax.broadcasted_iota(jnp.int32, (256, 256), 0)
    col_p = lax.broadcasted_iota(jnp.int32, (256, 256), 1)
    perm = one_hot(jnp.where(row_p < 128, 2 * row_p, 2 * row_p - 255) == col_p)

    def split(i, carry):
        both = gu_raw[pl.ds(pl.multiple_of(i * 256, 256), 256)]
        out = jnp.dot(perm, both, preferred_element_type=F32).astype(BF)
        rows = pl.ds(pl.multiple_of(i * 128, 128), 128)
        w_in[rows, 0:128] = out[0:128]
        w_in[rows, 128:256] = out[128:256]
        return carry

    lax.fori_loop(0, D // 128, split, 0)

    lane_r = lax.broadcasted_iota(jnp.int32, (128, 128), 0)
    lane_c = lax.broadcasted_iota(jnp.int32, (128, 128), 1)
    same = (lane_r >= 16) == (lane_c >= 16)
    earlier = one_hot((lane_r < lane_c) & same & (lane_c < 32) & (lane_r < 32))

    def routes(zz, yy):
        both = (
            keys[zz, yy, POOL_DEV:BLK, 512:WIDE].astype(F32)
            + keys[zz, yy, BLK + POOL_DEV : 2 * BLK, 512:WIDE].astype(F32)
        )
        shares = jnp.where(lane16 < 32, pltpu.roll(both, 64, 1), 0.0)
        chosen = shares > 0.0
        rank = jnp.dot(one_hot(chosen), earlier, preferred_element_type=F32)
        slot = jnp.where(chosen, rank + jnp.where(lane16 >= 16, float(CAP), 0.0), -1.0)
        return shares, slot

    row48 = lax.broadcasted_iota(jnp.int32, (ROWS, 128), 0)
    slot48 = jnp.where(row48 >= SLOTS, row48 - SLOTS, row48).astype(F32)
    _, own_slot = routes(z, y)
    for e in range(4):
        hit = own_slot[e : e + 1] == slot48
        d_top[e * ROWS : (e + 1) * ROWS] = one_hot(hit & (row48 < SLOTS))
        d_bot[e * ROWS : (e + 1) * ROWS] = one_hot(hit & (row48 >= SLOTS))

    for k, zz in enumerate(order):
        arrived(r_opp.at[k], ry_r.at[k])
        part[yp, zz] = (part[yp, zz].astype(F32) + r_opp[k].astype(F32)).astype(BF)
        send(part.at[yp, zz], r_rel.at[k], ry_s.at[8 + k], ry_r.at[8 + k], y_plus)

    def column_sum(k):
        arrived(r_pure.at[k], ry_r.at[4 + k])
        arrived(r_rel.at[k], ry_r.at[8 + k])
        return part[y, order[k]].astype(F32) + r_rel[k].astype(F32) + r_pure[k].astype(F32)

    z_out[0] = column_sum(0).astype(BF)
    send(z_out.at[0], z_opp, rz_s.at[0], rz_r.at[0], z_plus)
    z_out[1] = column_sum(1).astype(BF)
    send(z_out.at[1], z_pure, rz_s.at[1], rz_r.at[1], z_minus)
    ahead = column_sum(2)
    arrived(z_opp, rz_r.at[0])
    z_out[2] = (ahead + z_opp[...].astype(F32)).astype(BF)
    send(z_out.at[2], z_rel, rz_s.at[2], rz_r.at[2], z_plus)
    mid[...] = column_sum(3)

    loads[5].wait()
    loads[6].wait()
    arrived(res.at[1 - c], w_r.at[2])
    arrived(z_pure, rz_r.at[1])
    arrived(z_rel, rz_r.at[2])
    middle = mid[...] + z_pure[...].astype(F32) + z_rel[...].astype(F32)
    middle = middle + res[...].reshape(32, HALF).astype(F32)
    mid[...] = middle
    ss[0] = jnp.broadcast_to(jnp.sum(middle * middle, axis=1, keepdims=True), (32, 128))
    send(ss.at[0], ss.at[1], ss_s.at[0], ss_r.at[0], twin)
    arrived(ss.at[1], ss_r.at[0])
    scale = lax.rsqrt((ss[0] + ss[1])[:, 0:1] * (1.0 / D) + 1e-06)
    normed[...] = (mid[...] * scale * gain[...]).astype(BF)

    for n in range(2):
        lo = n * 896
        out = jnp.dot(d_top[:, 0:32], normed[:, lo : lo + 896], preferred_element_type=F32)
        out = out + jnp.dot(d_bot[:, 0:32], normed[:, QUART + lo : QUART + lo + 896], preferred_element_type=F32)
        disp[:, :, lo : lo + 896] = out.astype(BF).reshape(4, ROWS, 896)

    def slab(zz, yy):
        return got.at[c, zz, yy]

    def moe_send(zz, yy, number, to):
        remote(slab(zz, yy), slab(zz, yy), moe_s.at[number], moe_r.at[zz, yy], to).start()

    def moe_twin(zz, yy, number):
        remote(slab(zz, yy), slab(zz, yy), moe_s.at[number], moe_x.at[zz, yy], twin).start()

    def moe_wait(zz, yy):
        arrived(slab(zz, yy), moe_r.at[zz, yy])

    def moe_column(zz, number):
        moe_send(zz, y, number, y_plus)
        moe_send(zz, y, number + 1, y_minus)
        moe_twin(zz, y, number + 2)

    remote(disp.at[zo], relay, moe_s.at[0], rel_r.at[0], z_plus).start()
    remote(disp.at[zp], slab(z, y), moe_s.at[1], moe_r.at[z, y], z_plus).start()
    remote(disp.at[zm], slab(z, y), moe_s.at[2], moe_r.at[z, y], z_minus).start()
    got[c, z, y] = disp[z]
    moe_column(z, 4)
    arrived(relay, rel_r.at[0])
    remote(relay, slab(zm, y), moe_s.at[3], moe_r.at[zm, y], z_plus).start()
    moe_wait(zm, y)
    moe_column(zm, 7)
    moe_wait(zp, y)
    moe_column(zp, 10)
    moe_wait(zo, y)
    moe_column(zo, 13)

    def moe_near(t, carry):
        zz = (z - d * t + 8) % 4
        moe_wait(zz, ym)
        moe_send(zz, ym, 16 + t, y_plus)
        moe_twin(zz, ym, 20 + t)
        moe_wait(zz, yp)
        moe_twin(zz, yp, 24 + t)
        return carry

    def moe_far(t, carry):
        zz = (z - d * t + 8) % 4
        moe_wait(zz, yo)
        moe_twin(zz, yo, 28 + t)
        return carry

    slot24 = lax.broadcasted_iota(jnp.int32, (SLOTS, 128), 0).astype(F32)

    def experts(yy, number):
        for zz in (z, zm, zp, zo):
            arrived(got.at[1 - c, zz, yy], moe_x.at[zz, yy])
        top = jnp.zeros((4 * ROWS, 256), F32)
        bottom = jnp.zeros((4 * ROWS, 256), F32)
        for k in range(2):
            rows = got[k, :, yy].reshape(4 * ROWS, QUART)
            at = 2 * k * QUART
            top = top + jnp.dot(rows, w_in[at : at + QUART], preferred_element_type=F32)
            bottom = bottom + jnp.dot(rows, w_in[at + QUART : at + 2 * QUART], preferred_element_type=F32)
        for zz in range(4):
            at = zz * ROWS
            both = top[at : at + SLOTS] + bottom[at + SLOTS : at + ROWS]
            gate, upper = both[:, 0:128], both[:, 128:256]
            shares, slot = routes(zz, yy)
            mine_e = sub16 == z
            share = jnp.sum(jnp.where(mine_e, shares, 0.0), axis=0, keepdims=True)
            place_e = jnp.sum(jnp.where(mine_e, slot, 0.0), axis=0, keepdims=True)
            factor = jnp.sum(jnp.where(place_e == slot24, share, 0.0), axis=1, keepdims=True)
            hidden = factor * (gate * (1.0 / (1.0 + jnp.exp(-gate))) * upper)
            hid[c, yy, at : at + ROWS] = jnp.concatenate([hidden, hidden], axis=0).astype(BF)
        send(hid.at[c, yy], hid.at[c, yy], hid_s.at[number], hid_r.at[yy], twin)

    upper_half = (lax.broadcasted_iota(jnp.int32, (4, ROWS, 1), 1) < SLOTS).reshape(4 * ROWS, 1)

    def down(yy):
        arrived(hid.at[1 - c, yy], hid_r.at[yy])
        left, right = hid[0, yy], hid[1, yy]

        def column(n, carry):
            lo = pl.ds(pl.multiple_of(n * 256, 128), 256)
            hi = pl.ds(pl.multiple_of(QUART + n * 256, 128), 256)
            a = jnp.dot(left, wd[0, :, lo], preferred_element_type=F32)
            a = a + jnp.dot(right, wd[1, :, lo], preferred_element_type=F32)
            b = jnp.dot(left, wd[0, :, hi], preferred_element_type=F32)
            b = b + jnp.dot(right, wd[1, :, hi], preferred_element_type=F32)
            dpart[yy, :, :, lo] = jnp.where(upper_half, a, b).astype(BF).reshape(4, ROWS, 256)
            return carry

        lax.fori_loop(0, QUART // 256, column, 0)

    loads[4].wait()
    arrived(wd.at[1 - c], w_r.at[1])
    lax.fori_loop(0, 4, moe_near, 0)
    experts(y, 0)
    experts(ym, 1)
    experts(yp, 2)
    lax.fori_loop(0, 4, moe_far, 0)
    down(ym)
    for k, zz in enumerate(order):
        send(dpart.at[ym, zz], e_pure.at[k], ey_s.at[4 + k], ey_r.at[4 + k], y_minus)
    experts(yo, 3)
    down(yo)
    for k, zz in enumerate(order):
        send(dpart.at[yo, zz], e_opp.at[k], ey_s.at[k], ey_r.at[k], y_plus)
    down(yp)
    down(y)
    for k, zz in enumerate(order):
        arrived(e_opp.at[k], ey_r.at[k])
        dpart[yp, zz] = (dpart[yp, zz].astype(F32) + e_opp[k].astype(F32)).astype(BF)
        send(dpart.at[yp, zz], e_rel.at[k], ey_s.at[8 + k], ey_r.at[8 + k], y_plus)

    def plane_sum(k):
        arrived(e_pure.at[k], ey_r.at[4 + k])
        arrived(e_rel.at[k], ey_r.at[8 + k])
        s = dpart[y, order[k]].astype(F32) + e_rel[k].astype(F32) + e_pure[k].astype(F32)
        return s.astype(BF)

    e_out[0] = plane_sum(0)
    send(e_out.at[0], e_relay, ez_s.at[0], ez_r.at[0], z_plus)
    e_out[1] = plane_sum(1)
    send(e_out.at[1], e_got.at[z], ez_s.at[1], ez_r.at[1 + z], z_minus)
    e_out[2] = plane_sum(2)
    send(e_out.at[2], e_got.at[z], ez_s.at[2], ez_r.at[1 + z], z_plus)
    arrived(e_relay, ez_r.at[0])
    send(e_relay, e_got.at[zm], ez_s.at[3], ez_r.at[1 + zm], z_plus)
    e_got[z] = plane_sum(3)
    for zz in (zm, zp, zo):
        arrived(e_got.at[zz], ez_r.at[1 + zz])
    for n in range(2):
        rows = e_got[:, :, n * 896 : (n + 1) * 896].reshape(4 * ROWS, 896)
        for h, pick in enumerate((d_top, d_bot)):
            at = h * QUART + n * 896
            moe = lax.dot_general(pick[:, 0:32], rows, (((0,), (0,)), ((), ())), preferred_element_type=F32)
            o_stage[:, :, at : at + 896] = (mid[:, at : at + 896] + moe).astype(BF).reshape(2, TOK, 896)
    send(o_stage.at[1 - c], out_ref.at[:, half_c], o_s.at[0], o_r.at[0], twin)
    out_ref[:, half_c] = o_stage[c]
    arrived(out_ref.at[:, half_x], o_r.at[0])

    for k in range(1, NSEC):
        g = (sec - k + NSEC) % NSEC
        arrived(pages_ref.at[g], page_r.at[k - 1])
    for copy in sent:
        copy.wait_send()

    def key_done(i, carry):
        remote(block(z, y), block(z, y), key_s.at[i], key_r.at[z, y], twin).wait_send()
        return carry

    lax.fori_loop(0, N_KEY, key_done, 0)

    def moe_done(i, carry):
        remote(slab(z, y), slab(z, y), moe_s.at[i], moe_r.at[z, y], twin).wait_send()
        return carry

    lax.fori_loop(0, N_MOE, moe_done, 0)


def body(
    queries, stretch_latents, pool_latents, stretch_offset, value_up, out_proj, resid, norm_gain,
    expert_ids, route_weight, gate_up, down_proj, page_owner,
):
    anywhere = pl.BlockSpec(memory_space=pl.ANY)
    vmem = pl.BlockSpec(memory_space=pltpu.VMEM)
    smem = pl.BlockSpec(memory_space=pltpu.SMEM)
    V = pltpu.VMEM
    S = lambda *shape: pltpu.SemaphoreType.DMA(shape)
    scratch = [
        V((STRETCH, 2 * LATW), BF), V((2 * STRETCH, WIDE), BF), V((4, 4, 2 * BLK, WIDE), BF),
        V((2 * STRETCH, LAT), F32), V((2 * STRETCH, 128), F32), V((2 * STRETCH, 128), F32),
        V((2, 4, 4, 32, 256), BF), V((2, 256, HALF), BF), V((2, 128, HALF), BF),
        V((2 * D, 128), BF), V((D, 256), BF), V((2, LAT, HEAD_DIM), BF),
        V((2, TOK, HALF), BF), V((1, HALF), F32),
        V((NSEC, TOK, LATW), BF), V((4, 4, 32, HALF), BF),
        V((4, 32, HALF), BF), V((4, 32, HALF), BF), V((4, 32, HALF), BF),
        V((3, 32, HALF), BF), V((32, HALF), BF), V((32, HALF), BF), V((32, HALF), BF),
        V((32, HALF), F32), V((32, HALF), BF), V((2, 32, 128), F32),
        V((4 * ROWS, 128), BF), V((4 * ROWS, 128), BF),
        V((4, ROWS, QUART), BF), V((ROWS, QUART), BF), V((2, 4, 4, ROWS, QUART), BF),
        V((2, 4, 4 * ROWS, 128), BF),
        V((4, 4, ROWS, QUART), BF),
        V((4, ROWS, QUART), BF), V((4, ROWS, QUART), BF), V((4, ROWS, QUART), BF),
        V((3, ROWS, QUART), BF), V((ROWS, QUART), BF), V((4, ROWS, QUART), BF),
        V((2, TOK, HALF), BF),
        S(7), S(N_KEY), S(4, 4), S(4, 4), S(3), S(3), S(1), S(1), S(7), S(7),
        S(12), S(12), S(3), S(3), S(1), S(1), S(N_MOE), S(4, 4), S(4, 4), S(1), S(4), S(4),
        S(12), S(12), S(4), S(5), S(1), S(1),
    ]
    out, pages = pl.pallas_call(
        kernel,
        out_shape=(
            jax.ShapeDtypeStruct((TOK, D), BF),
            jax.ShapeDtypeStruct((NSEC, TOK, LATW), BF),
        ),
        in_specs=[smem, smem, anywhere, vmem, vmem, anywhere, anywhere, anywhere, anywhere, vmem, vmem, anywhere, anywhere],
        out_specs=(vmem, vmem),
        scratch_shapes=scratch,
        compiler_params=pltpu.CompilerParams(
            collective_id=0, has_side_effects=True, vmem_limit_bytes=60 * 1024 * 1024
        ),
    )(
        stretch_offset,
        page_owner[0],
        queries[0],
        stretch_latents[0],
        pool_latents[0],
        value_up[0],
        out_proj[0],
        resid[0],
        norm_gain,
        expert_ids[0].T,
        route_weight[0].T,
        gate_up[0, 0].reshape(2 * D, 128),
        down_proj[0, 0],
    )
    return out[None], pages.reshape(1, 1, NSEC, TOK * LATW)


def solution(mesh):
    placed = (
        P("section", None, "expert"),
        P("section", "expert", None),
        P("section", "expert", None),
        P("section"),
        P("section", "expert", None, None),
        P("section", "expert", None),
        P("section", "expert", None),
        P("section", None),
        P("section", "expert", None),
        P("section", "expert", None),
        P("section", "expert", None, None, None),
        P("section", "expert", None, None),
        P("section", "expert"),
    )
    return jax.shard_map(
        body,
        mesh=mesh,
        in_specs=placed,
        out_specs=(P("section", "expert", None), P("section", "expert", None, None)),
        check_vma=False,
    )
```

time: 426 us -> 175 us (0.41)
  waiting for transfers between devices: 302 us -> 0 us
  Pallas kernels: 0 us -> 169 us
  blocking collectives: 54.5 us -> 0 us
  matrix products: 33.5 us -> 0 us
  other arithmetic: 14.4 us -> 0 us
  between operations: 15.3 us -> 1.93 us
    reduce_scatter x2 -> x0, waiting for transfers between devices: 210 us -> none  [the longest x1 112 us: body(): lax.psum_scatter(jnp.dot(rows, out_proj[0], preferred_element_type=jnp.fl...]
    pallas_call x0 -> x1, Pallas kernels: none -> 169 us  [body(): pl.pallas_call(kernel, out_shape=(jax.ShapeDtypeStruct((TOK, D), BF), jax...]
    all_gather x2 -> x0, waiting for transfers between devices: 92.6 us -> none  [the longest x1 65.4 us: body(): piece = lax.all_gather(own_keys, 'expert', axis=0, tiled=True)]
    all_gather x1 -> x0, blocking collectives: 44.2 us -> none  [body(): lax.all_gather(table, 'expert', axis=0, tiled=True)]
    dot_general x6 -> x0, matrix products: 33.5 us -> none  [the longest x1 10.1 us: body(): jnp.einsum('qd,kd->qk', query_rows, piece, preferred_element_type=jnp.flo...]
    all_to_all x1 -> x0, blocking collectives: 10.4 us -> none  [body(): lax.all_to_all(outgoing, 'section', split_axis=1, concat_axis=1, tiled=True)]
    reduce_sum x4 -> x0, other arithmetic: 7.25 us -> none  [the longest x1 6.02 us: body(): denom = jnp.sum(probs, axis=1)]
  transfers between devices with their start and end apart: 4 -> 0, of which waited for: 4 -> 0; matrix products, arithmetic and copies ran while one was open for 2% -> 0% of each run, Pallas kernels for 0% -> 0%
where the time goes in v1:
time: 175 us; the launch traced here: 174 us
  Pallas kernels  169 us (97%)
  local copies, waits for them, and re-layouts  3.39 us (2%)
  between operations  1.93 us (1%)
    pallas_call x1, Pallas kernels, body(): pl.pallas_call(kernel, out_shape=(jax.ShapeDtypeStruct((TOK, D), BF), jax...  169 us

profile of v1, /device:TPU:1, one launch (start us, length us, event | category | flops | bytes accessed | tf_op | source)
XLA Modules:
  0.0 174.3 jit_solution(15787777490241513026)
XLA Ops:
  1.9 169.0 %shard_map.140 = (bf16[16,7168]{1,0:T(8,128)(2,1)}, bf16[8,16,576]{2,1,0:T(8,128)(2,1)}) custom-call(s32[1]{0:T(128)S(6)} %copy.16.offset_ref, s32[1]{0:T(128)} %bitcast.16.owner_ref, bf16[512,1152]{1,0:T(8,128)(2,1)} %bitcast.20, bf16[16,576]{1,0:T(8,128)(2,1)} %bitcast.25, bf16[96,576]{1,0:T(8,128)(2,1)} %bitcast.24, bf16[2,512,128]{2,1,0:T(8,128)(2,1)} %bitcast.21, ...), custom_call_target="tpu_custom_call" | custom-call | tf_op jit(solution)/shard_map/pallas_call | solution.py:543
  171.0 1.7 %reshape.7 = bf16[1,1,8,9216]{3,2,1,0:T(8,128)(2,1)} reshape(bf16[8,16,576]{2,1,0:T(8,128)(2,1)} %get-tuple-element.5) | data formatting | bytes 294912 | tf_op jit(solution)/shard_map/reshape | solution.py:570
  172.7 1.6 copy.18

commit v2 on v1

v2 whole, which is shorter than its diff:
```python
import math

import jax
import jax.numpy as jnp
from jax import lax
from jax.experimental import pallas as pl
from jax.experimental.pallas import tpu as pltpu
from jax.sharding import PartitionSpec as P

MESH = pl.DeviceIdType.MESH
BF = jnp.bfloat16
F32 = jnp.float32
D = 7168
HALF = D // 2
LAT = 512
LATW = 576
WIDE = 640
HEAD_DIM = 128
POOL_DEV = 96
TOK = 16
BLK = POOL_DEV + TOK
STRETCH = 512
CAP = 12
EIGHTH = D // 8
ROWS = 4 * CAP
TILE = 256
GROUP = 4 * 2 * BLK
NSEC = 8
NEG = -1e30
SCORE = math.log2(math.e) / math.sqrt(192.0)

N_KEY = 31
N_MOE = 31


def one_hot(mask):
    return jnp.where(mask, 1.0, 0.0).astype(BF)


def kernel(
    offset_ref, owner_ref, query_ref, stretch_ref, pool_ref, vup_ref, wo_ref, resid_ref, gain_ref,
    ids_ref, rw_ref, gu_ref, wd_ref,
    out_ref, pages_ref,
    q_raw, qs, keys, acc, ms, ls, ho, wo, wd, gu_raw, w_in, vup, res, gain,
    page_out, part, r_opp, r_rel, r_pure, z_out, z_opp, z_rel, z_pure,
    mid, normed, ss, d_sel, disp, got, hid,
    dpart, e_opp, e_rel, e_pure, e_out, e_got, o_stage,
    load_sem, key_s, key_r, key_x, w_s, w_r, ho_s, ho_r, page_s, page_r,
    ry_s, ry_r, rz_s, rz_r, ss_s, ss_r, moe_s, moe_r, moe_x, hid_s, hid_r,
    ey_s, ey_r, ez_s, ez_r, o_s, o_r,
):
    sec = lax.axis_index("section")
    me = lax.axis_index("expert")
    z = me // 8
    y = (me // 2) % 4
    c = me % 2
    d = 1 - 2 * c
    yp, ym, yo = (y + d + 4) % 4, (y - d + 4) % 4, (y + 2) % 4
    zp, zm, zo = (z + d + 4) % 4, (z - d + 4) % 4, (z + 2) % 4

    def dev(zz, yy, cc):
        return (sec, (zz * 4 + yy) * 2 + cc)

    y_plus, y_minus = dev(z, yp, c), dev(z, ym, c)
    z_plus, z_minus, z_far = dev(zp, y, c), dev(zm, y, c), dev(zo, y, c)
    twin = dev(z, y, 1 - c)
    barrier = pltpu.get_barrier_semaphore()
    for to in (y_plus, y_minus, z_plus, z_minus, z_far, twin):
        pl.semaphore_signal(barrier, inc=1, device_id=to, device_id_type=MESH)
    for k in range(1, NSEC):
        pl.semaphore_signal(barrier, inc=1, device_id=((sec + k) % NSEC, me), device_id_type=MESH)

    def remote(src, dst, s_sem, r_sem, to):
        return pltpu.make_async_remote_copy(
            src_ref=src, dst_ref=dst, send_sem=s_sem, recv_sem=r_sem, device_id=to, device_id_type=MESH
        )

    sent = []

    def send(src, dst, s_sem, r_sem, to):
        copy = remote(src, dst, s_sem, r_sem, to)
        copy.start()
        sent.append(copy)

    def arrived(dst, r_sem):
        remote(dst, dst, r_sem, r_sem, twin).wait_recv()

    half_c = pl.ds(pl.multiple_of(c * HALF, 128), HALF)
    half_x = pl.ds(pl.multiple_of((1 - c) * HALF, 128), HALF)

    wd_c = pl.ds(pl.multiple_of(c * 128, 128), 128)
    wd_x = pl.ds(pl.multiple_of((1 - c) * 128, 128), 128)
    loads = [
        pltpu.make_async_copy(query_ref, q_raw, load_sem.at[0]),
        pltpu.make_async_copy(vup_ref, vup, load_sem.at[1]),
        pltpu.make_async_copy(wo_ref.at[:, half_c], wo.at[c], load_sem.at[2]),
        pltpu.make_async_copy(gu_ref, gu_raw, load_sem.at[3]),
        pltpu.make_async_copy(wd_ref.at[:, half_c], wd.at[wd_c], load_sem.at[4]),
        pltpu.make_async_copy(resid_ref.at[:, half_c], res.at[c], load_sem.at[5]),
        pltpu.make_async_copy(gain_ref.at[:, half_c], gain, load_sem.at[6]),
    ]
    for load in loads:
        load.start()

    lane16 = lax.broadcasted_iota(jnp.int32, (16, 128), 1)
    sub16 = lax.broadcasted_iota(jnp.int32, (16, 128), 0)
    weights = rw_ref[...]
    total = weights[0:1] + weights[1:2]
    share0 = (2.827 * weights[0:1] / total).astype(BF).astype(F32)
    share1 = (2.827 * weights[1:2] / total).astype(BF).astype(F32)
    ids = ids_ref[...]
    which = lax.broadcasted_iota(jnp.int32, (16, TOK), 0)
    table = jnp.where(ids[0:1] == which, share0, 0.0) + jnp.where(ids[1:2] == which, share1, 0.0)
    place = one_hot(lane16 == sub16 + 64)
    tab = jnp.dot(table.astype(BF), place, preferred_element_type=F32).astype(BF)
    mine = pl.ds(pl.multiple_of(c * BLK, 16), BLK)
    first = pl.ds(pl.multiple_of(c * BLK, 16), POOL_DEV)
    last = pl.ds(pl.multiple_of(c * BLK + POOL_DEV, 16), TOK)
    keys[z, y, first, 512:WIDE] = jnp.zeros((POOL_DEV, 128), BF)
    keys[z, y, last, 512:WIDE] = tab
    keys[z, y, first, 0:LATW] = pool_ref[...]
    keys[z, y, last, 0:LATW] = stretch_ref[...]
    latents = stretch_ref[...]
    for g in range(NSEC):
        page_out[g] = jnp.where(owner_ref[0] == g, latents, jnp.zeros_like(latents))

    pl.semaphore_wait(barrier, 6 + NSEC - 1)

    def block(zz, yy):
        return keys.at[zz, yy, mine]

    def key_send(zz, yy, number, to):
        remote(block(zz, yy), block(zz, yy), key_s.at[number], key_r.at[zz, yy], to).start()

    def key_twin(zz, yy, number):
        remote(block(zz, yy), block(zz, yy), key_s.at[number], key_x.at[zz, yy], twin).start()

    def key_wait(zz, yy):
        arrived(block(zz, yy), key_r.at[zz, yy])

    def key_twin_wait(zz, yy):
        theirs = keys.at[zz, yy, pl.ds(pl.multiple_of((1 - c) * BLK, 16), BLK)]
        arrived(theirs, key_x.at[zz, yy])

    key_send(z, y, 2, z_plus)
    key_send(z, y, 3, z_minus)
    key_send(z, y, 0, y_plus)
    key_send(z, y, 1, y_minus)
    key_twin(z, y, 4)
    send(wo_ref.at[:, half_x], wo.at[c], w_s.at[0], w_r.at[0], twin)
    send(wd_ref.at[:, half_x], wd.at[wd_c], w_s.at[1], w_r.at[1], twin)
    send(resid_ref.at[:, half_x], res.at[c], w_s.at[2], w_r.at[2], twin)
    for k in range(1, NSEC):
        g = (sec + k) % NSEC
        send(page_out.at[g], pages_ref.at[sec], page_s.at[k - 1], page_r.at[k - 1], (g, me))
    pages_ref[sec] = page_out[sec]

    loads[0].wait()
    lane = lax.broadcasted_iota(jnp.int32, (STRETCH, WIDE), 1)
    head0 = jnp.where(lane < LATW, q_raw[:, 0:WIDE], jnp.zeros((), BF)).reshape(4, 4, 32, WIDE)
    row_i = lax.broadcasted_iota(jnp.int32, (WIDE, WIDE), 0)
    col_i = lax.broadcasted_iota(jnp.int32, (WIDE, WIDE), 1)
    shift = one_hot((row_i == col_i + 64) & (col_i < LATW))
    head1 = jnp.dot(q_raw[:, 512:1152], shift, preferred_element_type=F32).astype(BF).reshape(4, 4, 32, WIDE)
    for t in range(4):
        qs[t, 0:128] = head0[:, t].reshape(128, WIDE)
        qs[t, 128:256] = head1[:, t].reshape(128, WIDE)
    acc[...] = jnp.zeros_like(acc)
    ls[...] = jnp.zeros_like(ls)
    ms[...] = jnp.full(ms.shape, NEG, F32)

    row_p = lax.broadcasted_iota(jnp.int32, (256, 256), 0)
    col_p = lax.broadcasted_iota(jnp.int32, (256, 256), 1)
    perm = one_hot(jnp.where(row_p < 128, 2 * row_p, 2 * row_p - 255) == col_p)

    def split(i, carry):
        for k in range(4):
            both = gu_raw[pl.ds(pl.multiple_of(i * 1024 + k * 256, 256), 256)]
            out = jnp.dot(perm, both, preferred_element_type=F32).astype(BF)
            rows = pl.ds(pl.multiple_of(i * 512 + k * 128, 128), 128)
            w_in[rows, 0:128] = out[0:128]
            w_in[rows, 128:256] = out[128:256]
        return carry

    def own_column(zz, number):
        key_send(zz, y, number, y_plus)
        key_send(zz, y, number + 1, y_minus)
        key_twin(zz, y, number + 2)

    def key_column(zz, number):
        key_wait(zz, y)
        own_column(zz, number)

    def key_behind(zz, i):
        key_wait(zz, ym)
        key_send(zz, ym, 15 + i, y_plus)
        key_twin(zz, ym, 19 + i)

    def key_ahead(zz, i):
        key_wait(zz, yp)
        key_twin(zz, yp, 23 + i)

    def key_far(zz, i):
        key_wait(zz, yo)
        key_twin(zz, yo, 27 + i)

    def key_ready(blocks):
        for zz, yy in blocks:
            key_twin_wait(zz, yy)

    first_blocks = ((z, y), (z, ym), (z, yp), (zm, y))
    second_blocks = ((zp, y), (zo, y), (z, yo), (zm, ym))
    third_blocks = ((zm, yp), (zp, ym), (zp, yp), (zm, yo))
    last_blocks = ((zo, ym), (zo, yp), (zp, yo), (zo, yo))
    offset = offset_ref[0]

    def attend(blocks, tiles):
        r = lax.broadcasted_iota(jnp.int32, (1, GROUP), 1)
        number = (r >= 2 * BLK).astype(jnp.int32) + (r >= 4 * BLK).astype(jnp.int32) + (r >= 6 * BLK).astype(jnp.int32)
        r = r - number * (2 * BLK)
        cc = (r >= BLK).astype(jnp.int32)
        r = r - cc * BLK
        owner = jnp.zeros_like(r)
        for k, (zz, yy) in enumerate(blocks):
            owner = jnp.where(number == k, zz * 8 + yy * 2 + cc, owner)
        seen = jnp.where(owner * POOL_DEV + r < offset, -1, 1 << 20)
        limit = jnp.where(r < POOL_DEV, seen, owner * TOK + r - POOL_DEV)
        q = lax.broadcasted_iota(jnp.int32, (TILE, 1), 0)
        q = jnp.where(q >= 128, q - 128, q)
        piece = (q >= 32).astype(jnp.int32) + (q >= 64).astype(jnp.int32) + (q >= 96).astype(jnp.int32)
        q = q + 96 * piece
        results = []
        for t in tiles:
            part_keys = jnp.concatenate([keys[zz, yy] for zz, yy in blocks], axis=0)
            s = lax.dot_general(qs[t], part_keys, (((1,), (1,)), ((), ())), preferred_element_type=F32)
            s = jnp.where(limit <= q + 32 * t, s * SCORE, NEG)
            old = ms[t]
            new = jnp.maximum(old, jnp.max(s, axis=1, keepdims=True))
            p = jnp.exp2(s - new[:, 0:1])
            alpha = jnp.exp2(old - new)
            total = ls[t] * alpha + jnp.sum(p, axis=1, keepdims=True)
            add = jnp.dot(p.astype(BF), part_keys[:, 0:LAT], preferred_element_type=F32)
            results.append((new, total, acc[t] * alpha[:, 0:1] + add))
        for t, (new, total, mixed) in zip(tiles, results):
            ms[t] = new
            ls[t] = total
            acc[t] = mixed

    def finish(t, number):
        attend(last_blocks, (t,))
        latent = (acc[t] / ls[t][:, 0:1]).astype(BF)
        for h in range(2):
            head = jnp.dot(latent[h * 128 : h * 128 + 128], vup[h], preferred_element_type=F32).astype(BF)
            ho[c, t, :, h * HEAD_DIM : (h + 1) * HEAD_DIM] = head
        send(ho.at[c, t], ho.at[c, t], ho_s.at[number], ho_r.at[t], twin)

    def project(yy):
        arrived(ho.at[1 - c, yy], ho_r.at[yy])
        left, right = ho[0, yy], ho[1, yy]

        def column(n, carry):
            cols = pl.ds(pl.multiple_of(n * 896, 128), 896)
            out = jnp.dot(left, wo[0, :, cols], preferred_element_type=F32)
            out = out + jnp.dot(right, wo[1, :, cols], preferred_element_type=F32)
            part[yy, :, :, cols] = out.astype(BF).reshape(4, 32, 896)
            return carry

        lax.fori_loop(0, 4, column, 0)

    order = (zo, zm, zp, z)

    def piece(yy, k, h):
        return part.at[yy, order[k], pl.ds(h * TOK, TOK)]

    def opposite(h, k):
        send(piece(yo, k, h), r_opp.at[h, k], ry_s.at[h, k], ry_r.at[h, k], y_plus)

    def behind(h, k):
        send(piece(ym, k, h), r_pure.at[h, k], ry_s.at[h, 4 + k], ry_r.at[h, 4 + k], y_minus)

    def onward(h, k):
        arrived(r_opp.at[h, k], ry_r.at[h, k])
        at = piece(yp, k, h)
        at[...] = (at[...].astype(F32) + r_opp[h, k].astype(F32)).astype(BF)
        send(at, r_rel.at[h, k], ry_s.at[h, 8 + k], ry_r.at[h, 8 + k], y_plus)

    def column_sum(h, k):
        arrived(r_pure.at[h, k], ry_r.at[h, 4 + k])
        arrived(r_rel.at[h, k], ry_r.at[h, 8 + k])
        return piece(y, k, h)[...].astype(F32) + r_rel[h, k].astype(F32) + r_pure[h, k].astype(F32)

    lane_r = lax.broadcasted_iota(jnp.int32, (128, 128), 0)
    lane_c = lax.broadcasted_iota(jnp.int32, (128, 128), 1)
    earlier = one_hot((lane_r < lane_c) & (lane_c < TOK))

    def routes(h, zz, yy):
        at = h * BLK + POOL_DEV
        tail = keys[zz, yy, at : at + TOK, 512:WIDE].astype(F32)
        shares = jnp.where(lane16 < TOK, pltpu.roll(tail, 64, 1), 0.0)
        chosen = shares > 0.0
        rank = jnp.dot(one_hot(chosen), earlier, preferred_element_type=F32)
        return shares, jnp.where(chosen, rank, -1.0)

    def quarter_of(r):
        return jnp.where(r < 32, jnp.right_shift(r, 3), jnp.right_shift(r - 32, 2))

    def slot_of(r):
        return jnp.where(r < 32, jnp.bitwise_and(r, 7), 8 + jnp.bitwise_and(r, 3))

    row48 = lax.broadcasted_iota(jnp.int32, (ROWS, 128), 0)
    slot48 = slot_of(row48).astype(F32)
    quarter48 = quarter_of(row48)
    row16 = jnp.where(sub16 < 8, sub16, 8 + jnp.bitwise_and(sub16, 3)).astype(F32)
    quarter_all = quarter_of(lax.broadcasted_iota(jnp.int32, (4, ROWS, 1), 1)).reshape(4 * ROWS, 1)

    def pick_rows():
        for h in range(2):
            _, own_slot = routes(h, z, y)
            for e in range(4):
                hit = own_slot[e : e + 1] == slot48
                for j in range(4):
                    d_sel[h, j, e * ROWS : (e + 1) * ROWS] = one_hot(hit & (quarter48 == j))

    def z_first(h):
        z_out[h, 0] = column_sum(h, 0).astype(BF)
        send(z_out.at[h, 0], z_opp.at[h], rz_s.at[h, 0], rz_r.at[h, 0], z_plus)

    def z_second(h):
        z_out[h, 1] = column_sum(h, 1).astype(BF)
        send(z_out.at[h, 1], z_pure.at[h], rz_s.at[h, 1], rz_r.at[h, 1], z_minus)

    def z_third(h):
        ahead = column_sum(h, 2)
        arrived(z_opp.at[h], rz_r.at[h, 0])
        z_out[h, 2] = (ahead + z_opp[h].astype(F32)).astype(BF)
        send(z_out.at[h, 2], z_rel.at[h], rz_s.at[h, 2], rz_r.at[h, 2], z_plus)

    def norm(h):
        middle = column_sum(h, 3) + res[h].astype(F32)
        arrived(z_pure.at[h], rz_r.at[h, 1])
        arrived(z_rel.at[h], rz_r.at[h, 2])
        middle = middle + z_pure[h].astype(F32) + z_rel[h].astype(F32)
        mid[h] = middle
        ss[h, 0] = jnp.broadcast_to(jnp.sum(middle * middle, axis=1, keepdims=True), (TOK, 128))
        send(ss.at[h, 0], ss.at[h, 1], ss_s.at[h], ss_r.at[h], twin)

    def slab(h, zz, yy):
        return got.at[h, c, zz, yy]

    def moe_send(h, zz, yy, number, to):
        remote(slab(h, zz, yy), slab(h, zz, yy), moe_s.at[h, number], moe_r.at[h, zz, yy], to).start()

    def moe_twin(h, zz, yy, number):
        remote(slab(h, zz, yy), slab(h, zz, yy), moe_s.at[h, number], moe_x.at[h, zz, yy], twin).start()

    def moe_wait(h, zz, yy):
        arrived(slab(h, zz, yy), moe_r.at[h, zz, yy])

    def moe_column(h, zz, number):
        moe_send(h, zz, y, number, y_plus)
        moe_send(h, zz, y, number + 1, y_minus)
        moe_twin(h, zz, y, number + 2)

    def dispatch(h):
        arrived(ss.at[h, 1], ss_r.at[h])
        scale = lax.rsqrt((ss[h, 0] + ss[h, 1])[:, 0:1] * (1.0 / D) + 1e-06)
        normed[h] = (mid[h] * scale * gain[...]).astype(BF)
        out = jnp.zeros((4 * ROWS, EIGHTH), F32)
        for j in range(4):
            cols = normed[h, :, j * EIGHTH : (j + 1) * EIGHTH]
            out = out + jnp.dot(d_sel[h, j, :, 0:TOK], cols, preferred_element_type=F32)
        disp[h] = out.astype(BF).reshape(4, ROWS, EIGHTH)
        remote(disp.at[h, zp], slab(h, z, y), moe_s.at[h, 1], moe_r.at[h, z, y], z_plus).start()
        remote(disp.at[h, zm], slab(h, z, y), moe_s.at[h, 2], moe_r.at[h, z, y], z_minus).start()
        remote(disp.at[h, zo], slab(h, z, y), moe_s.at[h, 0], moe_r.at[h, z, y], z_far).start()
        got[h, c, z, y] = disp[h, z]
        moe_column(h, z, 3)

    def moe_spread(h, zz, number):
        moe_wait(h, zz, y)
        moe_column(h, zz, number)

    def moe_behind(h, zz, i):
        moe_wait(h, zz, ym)
        moe_send(h, zz, ym, 15 + i, y_plus)
        moe_twin(h, zz, ym, 19 + i)

    def moe_ahead(h, zz, i):
        moe_wait(h, zz, yp)
        moe_twin(h, zz, yp, 23 + i)

    def moe_far(h, zz, i):
        moe_wait(h, zz, yo)
        moe_twin(h, zz, yo, 27 + i)

    def experts(h, yy, number):
        for zz in (z, zm, zp, zo):
            arrived(got.at[h, 1 - c, zz, yy], moe_x.at[h, zz, yy])
        first_rows = got[h, 0, :, yy].reshape(4 * ROWS, EIGHTH)
        second_rows = got[h, 1, :, yy].reshape(4 * ROWS, EIGHTH)
        picked = jnp.zeros((4 * ROWS, 256), F32)
        for j in range(4):
            at = j * EIGHTH
            out = jnp.dot(first_rows, w_in[at : at + EIGHTH], preferred_element_type=F32)
            out = out + jnp.dot(second_rows, w_in[HALF + at : HALF + at + EIGHTH], preferred_element_type=F32)
            picked = jnp.where(quarter_all == j, out, picked)
        for zz in range(4):
            at = zz * ROWS
            head = picked[at : at + 8] + picked[at + 8 : at + 16] + picked[at + 16 : at + 24] + picked[at + 24 : at + 32]
            tail = picked[at + 32 : at + 40] + picked[at + 40 : at + 48]
            tail = tail + pltpu.roll(tail, 4, 0)
            both = jnp.concatenate([head, tail], axis=0)
            gate, upper = both[:, 0:128], both[:, 128:256]
            shares, slot = routes(h, zz, yy)
            mine_e = sub16 == z
            share = jnp.sum(jnp.where(mine_e, shares, 0.0), axis=0, keepdims=True)
            place_e = jnp.sum(jnp.where(mine_e, slot, 0.0), axis=0, keepdims=True)
            factor = jnp.sum(jnp.where(place_e == row16, share, 0.0), axis=1, keepdims=True)
            hidden = factor * (gate * (1.0 / (1.0 + jnp.exp(-gate))) * upper)
            low, high = hidden[0:8], hidden[8:16]
            hid[h, yy, at : at + ROWS, wd_c] = jnp.concatenate([low, low, low, low, high, high], axis=0).astype(BF)
        here = hid.at[h, yy, :, wd_c]
        remote(here, here, hid_s.at[h, number], hid_r.at[h, yy], twin).start()

    def down(h, yy):
        arrived(hid.at[h, yy, :, wd_x], hid_r.at[h, yy])
        rows = hid[h, yy]
        out = jnp.zeros((4 * ROWS, EIGHTH), F32)
        for j in range(4):
            term = jnp.dot(rows, wd[:, j * EIGHTH : (j + 1) * EIGHTH], preferred_element_type=F32)
            out = jnp.where(quarter_all == j, term, out)
        dpart[h, yy] = out.astype(BF).reshape(4, ROWS, EIGHTH)

    def e_behind(h, k):
        send(dpart.at[h, ym, order[k]], e_pure.at[h, k], ey_s.at[h, 4 + k], ey_r.at[h, 4 + k], y_minus)

    def e_opposite(h, k):
        send(dpart.at[h, yo, order[k]], e_opp.at[h, k], ey_s.at[h, k], ey_r.at[h, k], y_plus)

    def e_onward(h, k):
        arrived(e_opp.at[h, k], ey_r.at[h, k])
        dpart[h, yp, order[k]] = (dpart[h, yp, order[k]].astype(F32) + e_opp[h, k].astype(F32)).astype(BF)
        send(dpart.at[h, yp, order[k]], e_rel.at[h, k], ey_s.at[h, 8 + k], ey_r.at[h, 8 + k], y_plus)

    def plane_sum(h, k):
        arrived(e_pure.at[h, k], ey_r.at[h, 4 + k])
        arrived(e_rel.at[h, k], ey_r.at[h, 8 + k])
        s = dpart[h, y, order[k]].astype(F32) + e_rel[h, k].astype(F32) + e_pure[h, k].astype(F32)
        return s.astype(BF)

    def back_first(h):
        e_out[h, 0] = plane_sum(h, 0)
        send(e_out.at[h, 0], e_got.at[h, z], ez_s.at[h, 0], ez_r.at[h, z], z_far)

    def back_second(h):
        e_out[h, 1] = plane_sum(h, 1)
        send(e_out.at[h, 1], e_got.at[h, z], ez_s.at[h, 1], ez_r.at[h, z], z_minus)

    def back_third(h):
        e_out[h, 2] = plane_sum(h, 2)
        send(e_out.at[h, 2], e_got.at[h, z], ez_s.at[h, 2], ez_r.at[h, z], z_plus)

    def combine(h):
        e_got[h, z] = plane_sum(h, 3)
        for zz in (zm, zp, zo):
            arrived(e_got.at[h, zz], ez_r.at[h, zz])
        rows = e_got[h].reshape(4 * ROWS, EIGHTH)
        for j in range(4):
            pick = d_sel[h, j, :, 0:TOK]
            moe = lax.dot_general(pick, rows, (((0,), (0,)), ((), ())), preferred_element_type=F32)
            at = j * EIGHTH
            o_stage[h, :, at : at + EIGHTH] = (mid[h, :, at : at + EIGHTH] + moe).astype(BF)

    loads[3].wait()
    lax.fori_loop(0, D // 512, split, 0)
    key_behind(z, 0)
    key_ahead(z, 0)
    key_wait(zm, y)
    key_send(zm, y, 5, z_plus)
    own_column(zm, 6)
    key_column(zp, 9)
    key_ready(first_blocks)
    attend(first_blocks, (2, 3))
    key_far(z, 0)
    attend(first_blocks, (0, 1))
    key_behind(zm, 1)
    key_column(zo, 12)
    key_ahead(zm, 1)
    key_behind(zp, 2)
    key_ahead(zp, 2)
    key_ready(second_blocks)
    attend(second_blocks, (2, 3))
    key_behind(zo, 3)
    key_far(zm, 1)
    attend(second_blocks, (0, 1))
    key_ahead(zo, 3)
    key_far(zp, 2)
    key_ready(third_blocks)
    attend(third_blocks, (0, 1))
    key_far(zo, 3)
    attend(third_blocks, (2, 3))
    key_ready(last_blocks)
    loads[1].wait()
    finish(yo, 3)
    finish(ym, 1)
    loads[2].wait()
    arrived(wo.at[1 - c], w_r.at[0])
    project(yo)
    opposite(1, 1)
    opposite(0, 1)
    opposite(1, 0)
    opposite(0, 0)
    opposite(1, 2)
    finish(y, 0)
    opposite(1, 3)
    pick_rows()
    opposite(0, 2)
    finish(yp, 2)
    project(yp)
    onward(1, 0)
    project(ym)
    behind(1, 0)
    onward(0, 0)
    behind(0, 0)
    behind(1, 1)
    onward(1, 1)
    behind(1, 2)
    onward(1, 2)
    behind(0, 2)
    behind(1, 3)
    project(y)
    onward(0, 2)
    onward(1, 3)
    onward(0, 1)
    behind(0, 1)
    behind(0, 3)
    opposite(0, 3)
    z_first(1)
    z_first(0)
    z_second(1)
    z_third(1)
    z_third(0)
    loads[5].wait()
    loads[6].wait()
    arrived(res.at[1 - c], w_r.at[2])
    norm(1)
    z_second(0)
    dispatch(1)
    onward(0, 3)
    moe_behind(1, z, 0)
    moe_ahead(1, z, 0)
    norm(0)
    moe_spread(1, zm, 6)
    moe_far(1, z, 0)
    dispatch(0)
    moe_spread(1, zp, 9)
    moe_behind(1, zm, 1)
    moe_ahead(1, zm, 1)
    moe_behind(0, z, 0)
    moe_ahead(0, z, 0)
    moe_spread(1, zo, 12)
    moe_behind(1, zp, 2)
    moe_spread(0, zm, 6)
    moe_ahead(1, zp, 2)
    experts(1, y, 0)
    moe_spread(0, zp, 9)
    moe_far(0, z, 0)
    moe_far(1, zm, 1)
    loads[4].wait()
    arrived(wd.at[wd_x], w_r.at[1])
    down(1, y)
    moe_behind(1, zo, 3)
    moe_ahead(1, zo, 3)
    moe_far(1, zp, 2)
    experts(1, yp, 2)
    moe_spread(0, zo, 12)
    moe_ahead(0, zm, 1)
    experts(1, ym, 1)
    moe_behind(0, zp, 2)
    moe_ahead(0, zp, 2)
    down(1, ym)
    e_behind(1, 2)
    e_behind(1, 1)
    e_behind(1, 0)
    moe_far(1, zo, 3)
    moe_behind(0, zm, 1)
    e_behind(1, 3)
    moe_behind(0, zo, 3)
    down(1, yp)
    moe_ahead(0, zo, 3)
    experts(1, yo, 3)
    experts(0, yp, 2)
    down(1, yo)
    e_opposite(1, 2)
    e_opposite(1, 1)
    e_opposite(1, 3)
    e_opposite(1, 0)
    moe_far(0, zp, 2)
    experts(0, ym, 1)
    moe_far(0, zm, 1)
    down(0, ym)
    e_behind(0, 2)
    e_behind(0, 3)
    moe_far(0, zo, 3)
    down(0, yp)
    e_behind(0, 1)
    e_onward(1, 2)
    e_behind(0, 0)
    e_onward(1, 1)
    experts(0, yo, 3)
    e_onward(1, 3)
    e_onward(1, 0)
    experts(0, y, 0)
    down(0, yo)
    e_opposite(0, 2)
    e_opposite(0, 0)
    e_opposite(0, 1)
    e_opposite(0, 3)
    down(0, y)
    back_third(1)
    back_second(1)
    back_first(1)
    e_onward(0, 2)
    e_onward(0, 0)
    e_onward(0, 1)
    e_onward(0, 3)
    back_third(0)
    back_first(0)
    back_second(0)
    combine(1)
    combine(0)
    send(o_stage.at[1 - c], out_ref.at[:, half_c], o_s.at[0], o_r.at[0], twin)
    out_ref[:, half_c] = o_stage[c]
    arrived(out_ref.at[:, half_x], o_r.at[0])

    for k in range(1, NSEC):
        g = (sec - k + NSEC) % NSEC
        arrived(pages_ref.at[g], page_r.at[k - 1])
    for copy in sent:
        copy.wait_send()

    def key_done(i, carry):
        remote(block(z, y), block(z, y), key_s.at[i], key_r.at[z, y], twin).wait_send()
        return carry

    lax.fori_loop(0, N_KEY, key_done, 0)

    def moe_done(i, carry):
        for h in range(2):
            remote(slab(h, z, y), slab(h, z, y), moe_s.at[h, i], moe_r.at[h, z, y], twin).wait_send()
        return carry

    lax.fori_loop(0, N_MOE, moe_done, 0)

    def hid_done(i, carry):
        for h in range(2):
            here = hid.at[h, i, :, wd_c]
            remote(here, here, hid_s.at[h, i], hid_r.at[h, i], twin).wait_send()
        return carry

    lax.fori_loop(0, 4, hid_done, 0)


def body(
    queries, stretch_latents, pool_latents, stretch_offset, value_up, out_proj, resid, norm_gain,
    expert_ids, route_weight, gate_up, down_proj, page_owner,
):
    anywhere = pl.BlockSpec(memory_space=pl.ANY)
    vmem = pl.BlockSpec(memory_space=pltpu.VMEM)
    smem = pl.BlockSpec(memory_space=pltpu.SMEM)
    V = pltpu.VMEM
    S = lambda *shape: pltpu.SemaphoreType.DMA(shape)
    scratch = [
        V((STRETCH, 2 * LATW), BF), V((4, TILE, WIDE), BF), V((4, 4, 2 * BLK, WIDE), BF),
        V((4, TILE, LAT), F32), V((4, TILE, 128), F32), V((4, TILE, 128), F32),
        V((2, 4, 128, 256), BF), V((2, 256, HALF), BF), V((256, HALF), BF),
        V((2 * D, 128), BF), V((D, 256), BF), V((2, LAT, HEAD_DIM), BF),
        V((2, TOK, HALF), BF), V((1, HALF), F32),
        V((NSEC, TOK, LATW), BF), V((4, 4, 32, HALF), BF),
        V((2, 4, TOK, HALF), BF), V((2, 4, TOK, HALF), BF), V((2, 4, TOK, HALF), BF),
        V((2, 3, TOK, HALF), BF), V((2, TOK, HALF), BF), V((2, TOK, HALF), BF), V((2, TOK, HALF), BF),
        V((2, TOK, HALF), F32), V((2, TOK, HALF), BF), V((2, 2, TOK, 128), F32),
        V((2, 4, 4 * ROWS, 128), BF),
        V((2, 4, ROWS, EIGHTH), BF), V((2, 2, 4, 4, ROWS, EIGHTH), BF),
        V((2, 4, 4 * ROWS, 256), BF),
        V((2, 4, 4, ROWS, EIGHTH), BF),
        V((2, 4, ROWS, EIGHTH), BF), V((2, 4, ROWS, EIGHTH), BF), V((2, 4, ROWS, EIGHTH), BF),
        V((2, 3, ROWS, EIGHTH), BF), V((2, 4, ROWS, EIGHTH), BF),
        V((2, TOK, HALF), BF),
        S(7), S(N_KEY), S(4, 4), S(4, 4), S(3), S(3), S(4), S(4), S(7), S(7),
        S(2, 12), S(2, 12), S(2, 3), S(2, 3), S(2), S(2),
        S(2, N_MOE), S(2, 4, 4), S(2, 4, 4), S(2, 4), S(2, 4),
        S(2, 12), S(2, 12), S(2, 3), S(2, 4), S(1), S(1),
    ]
    out, pages = pl.pallas_call(
        kernel,
        out_shape=(
            jax.ShapeDtypeStruct((TOK, D), BF),
            jax.ShapeDtypeStruct((NSEC, TOK, LATW), BF),
        ),
        in_specs=[smem, smem, anywhere, vmem, vmem, anywhere, anywhere, anywhere, anywhere, vmem, vmem, anywhere, anywhere],
        out_specs=(vmem, vmem),
        scratch_shapes=scratch,
        compiler_params=pltpu.CompilerParams(
            collective_id=0, has_side_effects=True, vmem_limit_bytes=60 * 1024 * 1024
        ),
    )(
        stretch_offset,
        page_owner[0],
        queries[0],
        stretch_latents[0],
        pool_latents[0],
        value_up[0],
        out_proj[0],
        resid[0],
        norm_gain,
        expert_ids[0].T,
        route_weight[0].T,
        gate_up[0, 0].reshape(2 * D, 128),
        down_proj[0, 0],
    )
    return out[None], pages.reshape(1, 1, NSEC, TOK * LATW)


def solution(mesh):
    placed = (
        P("section", None, "expert"),
        P("section", "expert", None),
        P("section", "expert", None),
        P("section"),
        P("section", "expert", None, None),
        P("section", "expert", None),
        P("section", "expert", None),
        P("section", None),
        P("section", "expert", None),
        P("section", "expert", None),
        P("section", "expert", None, None, None),
        P("section", "expert", None, None),
        P("section", "expert"),
    )
    return jax.shard_map(
        body,
        mesh=mesh,
        in_specs=placed,
        out_specs=(P("section", "expert", None), P("section", "expert", None, None)),
        check_vma=False,
    )
```

time: 175 us -> 152 us (0.87)
  Pallas kernels: 169 us -> 147 us
    pallas_call x1, Pallas kernels: 169 us -> 147 us  [body(): pl.pallas_call(kernel, out_shape=(jax.ShapeDtypeStruct((TOK, D), BF), jax...]
where the time goes in v2:
time: 152 us
  Pallas kernels  147 us (97%)
  local copies, waits for them, and re-layouts  3.39 us (2%)
  between operations  1.94 us (1%)
    pallas_call x1, Pallas kernels, body(): pl.pallas_call(kernel, out_shape=(jax.ShapeDtypeStruct((TOK, D), BF), jax...  147 us

profile of v2, /device:TPU:1, one launch (start us, length us, event | category | flops | bytes accessed | tf_op | source)
XLA Modules:
  0.0 151.9 jit_solution(10239529130789512811)
XLA Ops:
  1.9 146.6 %shard_map.140 = (bf16[16,7168]{1,0:T(8,128)(2,1)}, bf16[8,16,576]{2,1,0:T(8,128)(2,1)}) custom-call(s32[1]{0:T(128)S(6)} %copy.16.offset_ref, s32[1]{0:T(128)} %bitcast.16.owner_ref, bf16[512,1152]{1,0:T(8,128)(2,1)} %bitcast.20, bf16[16,576]{1,0:T(8,128)(2,1)} %bitcast.25, bf16[96,576]{1,0:T(8,128)(2,1)} %bitcast.24, bf16[2,512,128]{2,1,0:T(8,128)(2,1)} %bitcast.21, ...), custom_call_target="tpu_custom_call" | custom-call | tf_op jit(solution)/shard_map/pallas_call | solution.py:695
  148.5 1.7 %reshape.7 = bf16[1,1,8,9216]{3,2,1,0:T(8,128)(2,1)} reshape(bf16[8,16,576]{2,1,0:T(8,128)(2,1)} %get-tuple-element.5) | data formatting | bytes 294912 | tf_op jit(solution)/shard_map/reshape | solution.py:722
  150.2 1.6 %copy.18 = bf16[1,16,7168]{2,1,0:T(8,128)(2,1)} copy(bf16[1,16,7168]{2,1,0:T(8,128)(2,1)} %bitcast.22) | data formatting | bytes 458752

commit v3 on v2

--- a/solution.py
+++ b/solution.py
@@ -229,22 +229,22 @@
         q = jnp.where(q >= 128, q - 128, q)
         piece = (q >= 32).astype(jnp.int32) + (q >= 64).astype(jnp.int32) + (q >= 96).astype(jnp.int32)
         q = q + 96 * piece
-        results = []
-        for t in tiles:
-            part_keys = jnp.concatenate([keys[zz, yy] for zz, yy in blocks], axis=0)
-            s = lax.dot_general(qs[t], part_keys, (((1,), (1,)), ((), ())), preferred_element_type=F32)
-            s = jnp.where(limit <= q + 32 * t, s * SCORE, NEG)
-            old = ms[t]
-            new = jnp.maximum(old, jnp.max(s, axis=1, keepdims=True))
-            p = jnp.exp2(s - new[:, 0:1])
-            alpha = jnp.exp2(old - new)
-            total = ls[t] * alpha + jnp.sum(p, axis=1, keepdims=True)
-            add = jnp.dot(p.astype(BF), part_keys[:, 0:LAT], preferred_element_type=F32)
-            results.append((new, total, acc[t] * alpha[:, 0:1] + add))
-        for t, (new, total, mixed) in zip(tiles, results):
-            ms[t] = new
-            ls[t] = total
-            acc[t] = mixed
+        span = len(tiles)
+        at = pl.ds(tiles[0], span)
+        part_keys = jnp.concatenate([keys[zz, yy] for zz, yy in blocks], axis=0)
+        token = jnp.concatenate([q + 32 * t for t in tiles], axis=0)
+        many = qs[at].reshape(span * TILE, WIDE)
+        s = lax.dot_general(many, part_keys, (((1,), (1,)), ((), ())), preferred_element_type=F32)
+        s = jnp.where(limit <= token, s * SCORE, NEG)
+        old = ms[at].reshape(span * TILE, 128)
+        new = jnp.maximum(old, jnp.max(s, axis=1, keepdims=True))
+        p = jnp.exp2(s - new[:, 0:1])
+        alpha = jnp.exp2(old - new)
+        ms[at] = new.reshape(span, TILE, 128)
+        total = ls[at].reshape(span * TILE, 128) * alpha + jnp.sum(p, axis=1, keepdims=True)
+        ls[at] = total.reshape(span, TILE, 128)
+        add = jnp.dot(p.astype(BF), part_keys[:, 0:LAT], preferred_element_type=F32)
+        acc[at] = (acc[at].reshape(span * TILE, LAT) * alpha[:, 0:1] + add).reshape(span, TILE, LAT)
 
     def finish(t, number):
         attend(last_blocks, (t,))
@@ -474,30 +474,30 @@
     loads[3].wait()
     lax.fori_loop(0, D // 512, split, 0)
     key_behind(z, 0)
-    key_ahead(z, 0)
     key_wait(zm, y)
     key_send(zm, y, 5, z_plus)
     own_column(zm, 6)
+    key_ahead(z, 0)
     key_column(zp, 9)
     key_ready(first_blocks)
-    attend(first_blocks, (2, 3))
-    key_far(z, 0)
     attend(first_blocks, (0, 1))
     key_behind(zm, 1)
+    key_far(z, 0)
+    attend(first_blocks, (2, 3))
     key_column(zo, 12)
+    key_behind(zp, 2)
     key_ahead(zm, 1)
-    key_behind(zp, 2)
     key_ahead(zp, 2)
+    key_far(zm, 1)
     key_ready(second_blocks)
     attend(second_blocks, (2, 3))
     key_behind(zo, 3)
-    key_far(zm, 1)
     attend(second_blocks, (0, 1))
     key_ahead(zo, 3)
     key_far(zp, 2)
+    key_far(zo, 3)
     key_ready(third_blocks)
     attend(third_blocks, (0, 1))
-    key_far(zo, 3)
     attend(third_blocks, (2, 3))
     key_ready(last_blocks)
     loads[1].wait()
@@ -506,127 +506,127 @@
     loads[2].wait()
     arrived(wo.at[1 - c], w_r.at[0])
     project(yo)
+    opposite(1, 0)
+    opposite(0, 2)
     opposite(1, 1)
     opposite(0, 1)
-    opposite(1, 0)
+    opposite(1, 2)
     opposite(0, 0)
-    opposite(1, 2)
+    pick_rows()
     finish(y, 0)
     opposite(1, 3)
-    pick_rows()
-    opposite(0, 2)
     finish(yp, 2)
     project(yp)
     onward(1, 0)
+    project(y)
     project(ym)
     behind(1, 0)
+    behind(0, 0)
+    onward(1, 2)
     onward(0, 0)
-    behind(0, 0)
+    onward(1, 1)
     behind(1, 1)
-    onward(1, 1)
     behind(1, 2)
-    onward(1, 2)
     behind(0, 2)
+    onward(0, 2)
     behind(1, 3)
-    project(y)
-    onward(0, 2)
+    behind(0, 1)
+    onward(0, 1)
+    opposite(0, 3)
     onward(1, 3)
-    onward(0, 1)
-    behind(0, 1)
     behind(0, 3)
-    opposite(0, 3)
     z_first(1)
     z_first(0)
     z_second(1)
     z_third(1)
     z_third(0)
+    z_second(0)
+    onward(0, 3)
     loads[5].wait()
     loads[6].wait()
     arrived(res.at[1 - c], w_r.at[2])
     norm(1)
-    z_second(0)
     dispatch(1)
-    onward(0, 3)
+    norm(0)
+    dispatch(0)
     moe_behind(1, z, 0)
     moe_ahead(1, z, 0)
-    norm(0)
     moe_spread(1, zm, 6)
+    moe_spread(1, zp, 9)
+    moe_behind(0, z, 0)
+    moe_ahead(0, z, 0)
     moe_far(1, z, 0)
-    dispatch(0)
-    moe_spread(1, zp, 9)
     moe_behind(1, zm, 1)
     moe_ahead(1, zm, 1)
-    moe_behind(0, z, 0)
-    moe_ahead(0, z, 0)
+    moe_behind(1, zp, 2)
     moe_spread(1, zo, 12)
-    moe_behind(1, zp, 2)
     moe_spread(0, zm, 6)
     moe_ahead(1, zp, 2)
+    moe_far(0, z, 0)
     experts(1, y, 0)
+    moe_far(1, zm, 1)
     moe_spread(0, zp, 9)
-    moe_far(0, z, 0)
-    moe_far(1, zm, 1)
+    moe_far(1, zp, 2)
     loads[4].wait()
     arrived(wd.at[wd_x], w_r.at[1])
     down(1, y)
     moe_behind(1, zo, 3)
     moe_ahead(1, zo, 3)
-    moe_far(1, zp, 2)
+    moe_behind(0, zm, 1)
     experts(1, yp, 2)
     moe_spread(0, zo, 12)
+    moe_behind(0, zp, 2)
+    experts(1, ym, 1)
+    moe_far(1, zo, 3)
+    experts(0, y, 0)
+    experts(1, yo, 3)
+    moe_behind(0, zo, 3)
+    down(1, ym)
+    e_behind(1, 1)
+    down(1, yo)
+    e_opposite(1, 1)
+    e_opposite(1, 0)
+    moe_ahead(0, zp, 2)
+    e_opposite(1, 2)
+    moe_far(0, zp, 2)
+    moe_ahead(0, zo, 3)
+    e_behind(1, 0)
+    down(1, yp)
+    moe_far(0, zm, 1)
+    e_behind(1, 2)
+    moe_far(0, zo, 3)
     moe_ahead(0, zm, 1)
-    experts(1, ym, 1)
-    moe_behind(0, zp, 2)
-    moe_ahead(0, zp, 2)
-    down(1, ym)
-    e_behind(1, 2)
-    e_behind(1, 1)
-    e_behind(1, 0)
-    moe_far(1, zo, 3)
-    moe_behind(0, zm, 1)
-    e_behind(1, 3)
-    moe_behind(0, zo, 3)
-    down(1, yp)
-    moe_ahead(0, zo, 3)
-    experts(1, yo, 3)
     experts(0, yp, 2)
-    down(1, yo)
-    e_opposite(1, 2)
-    e_opposite(1, 1)
-    e_opposite(1, 3)
-    e_opposite(1, 0)
-    moe_far(0, zp, 2)
-    experts(0, ym, 1)
-    moe_far(0, zm, 1)
-    down(0, ym)
-    e_behind(0, 2)
-    e_behind(0, 3)
-    moe_far(0, zo, 3)
-    down(0, yp)
-    e_behind(0, 1)
-    e_onward(1, 2)
-    e_behind(0, 0)
     e_onward(1, 1)
     experts(0, yo, 3)
-    e_onward(1, 3)
     e_onward(1, 0)
-    experts(0, y, 0)
+    e_onward(1, 2)
+    down(0, y)
     down(0, yo)
-    e_opposite(0, 2)
     e_opposite(0, 0)
     e_opposite(0, 1)
+    e_opposite(0, 2)
+    experts(0, ym, 1)
+    back_second(1)
+    down(0, ym)
+    back_third(1)
+    e_behind(0, 3)
+    e_behind(0, 0)
+    e_behind(0, 2)
+    down(0, yp)
+    e_onward(0, 0)
+    e_behind(0, 1)
+    e_onward(0, 1)
+    e_behind(1, 3)
+    back_first(1)
     e_opposite(0, 3)
-    down(0, y)
-    back_third(1)
-    back_second(1)
-    back_first(1)
     e_onward(0, 2)
-    e_onward(0, 0)
-    e_onward(0, 1)
+    e_opposite(1, 3)
+    back_first(0)
+    back_second(0)
     e_onward(0, 3)
     back_third(0)
-    back_first(0)
-    back_second(0)
+    e_onward(1, 3)
     combine(1)
     combine(0)
     send(o_stage.at[1 - c], out_ref.at[:, half_c], o_s.at[0], o_r.at[0], twin)

time: 152 us -> 153 us (level)
  no operation moved by 1% of the time
where the time goes in v3:
time: 153 us; the launch traced here: 152 us
  Pallas kernels  147 us (96%)
  local copies, waits for them, and re-layouts  3.39 us (2%)
  between operations  1.94 us (1%)
    pallas_call x1, Pallas kernels, body(): pl.pallas_call(kernel, out_shape=(jax.ShapeDtypeStruct((TOK, D), BF), jax...  147 us

profile of v3, /device:TPU:1, one launch (start us, length us, event | category | flops | bytes accessed | tf_op | source)
XLA Modules:
  0.0 152.2 jit_solution(14707717132457115471)
XLA Ops:
  1.9 146.9 %shard_map.140 = (bf16[16,7168]{1,0:T(8,128)(2,1)}, bf16[8,16,576]{2,1,0:T(8,128)(2,1)}) custom-call(s32[1]{0:T(128)S(6)} %copy.16.offset_ref, s32[1]{0:T(128)} %bitcast.16.owner_ref, bf16[512,1152]{1,0:T(8,128)(2,1)} %bitcast.20, bf16[16,576]{1,0:T(8,128)(2,1)} %bitcast.25, bf16[96,576]{1,0:T(8,128)(2,1)} %bitcast.24, bf16[2,512,128]{2,1,0:T(8,128)(2,1)} %bitcast.21, ...), custom_call_target="tpu_custom_call" | custom-call | tf_op jit(solution)/shard_map/pallas_call | solution.py:695
  148.8 1.7 %reshape.7 = bf16[1,1,8,9216]{3,2,1,0:T(8,128)(2,1)} reshape(bf16[8,16,576]{2,1,0:T(8,128)(2,1)} %get-tuple-element.5) | data formatting | bytes 294912 | tf_op jit(solution)/shard_map/reshape | solution.py:722
  150.6 1.6 %copy.18 = bf16[1,16,7168]{2,1,0:T(8,128)(2,1)} copy(bf16[1,16,7168]{2,1,0:T(8,128)(2,1)} %bitcast.22) | data formatting | bytes 458752
